TPU v7x, 32 devices: a whole 2x2x4 slice. The times are simulated.
32 devices in a mesh: row: 4 (over z), col: 8 (over y, x, core).
Axes of the slice: x: 2, y: 2, z: 4, core: 2. Of those that a mesh axis runs over, the one named last changes fastest.
Arguments:
- noise: float32 [2048, 2048], P(('row', 'col')), may hold values from -22 to 22
- data: float32 [8192, 2048], P(('col', 'row')), may hold values from -22 to 22
- times: float32 [2048], P(('row', 'col')), may hold values from 0 to 1
Outputs:
- path: float32 [2048, 2048], P(('row', 'col'))
- velocity: float32 [2048, 2048], P(('row', 'col'))
All inputs are finite; a program needn't handle non-finite values.
Results may differ from a plain program's by a relative error of at most 0.0003.
Values sent between devices are 32-bit elements; how exact they have to be, the bound alone decides.
A program may use at most 192 MiB of HBM per device.

v0:
```python
import math

import jax
import jax.numpy as jnp
from jax import lax
from jax.sharding import PartitionSpec as P

ITERS = 2


epsilon = 0.05
highest = lax.Precision.HIGHEST


def cost_block(rows, row_norms, cols, col_norms):
    cross = lax.dot_general(rows, cols, (((1,), (1,)), ((), ())), precision=highest)
    return (row_norms[:, None] + col_norms[None, :] - 2.0 * cross) / rows.shape[1]


def per_device(noise, data, times):
    rows_all = lax.all_gather(noise, "col", axis=0, tiled=True)
    cols_all = lax.all_gather(data, "row", axis=0, tiled=True)
    features = noise.shape[1]
    row_count = rows_all.shape[0]
    col_count = cols_all.shape[0]
    total_noise = row_count * lax.axis_size("row")
    total_data = col_count * lax.axis_size("col")
    block_rows = min(512, row_count)
    block_count = row_count // block_rows
    row_norms = jnp.sum(rows_all * rows_all, axis=1)
    col_norms = jnp.sum(cols_all * cols_all, axis=1)
    row_blocks = rows_all.reshape(block_count, block_rows, features)
    norm_blocks = row_norms.reshape(block_count, block_rows)

    def scores_rows(rows, norms, col_pot):
        return (col_pot[None, :] - cost_block(rows, norms, cols_all, col_norms)) / epsilon

    def scores_cols(rows, norms, pot_piece):
        return (pot_piece[:, None] - cost_block(rows, norms, cols_all, col_norms)) / epsilon

    col_pot = jnp.zeros((col_count,), jnp.float32)
    for step in range(ITERS):
        row_peaks = lax.map(
            lambda args: jnp.max(scores_rows(args[0], args[1], col_pot), axis=1),
            (row_blocks, norm_blocks),
        ).reshape(row_count)
        row_peaks = lax.pmax(row_peaks, "col")
        row_totals = lax.map(
            lambda args: jnp.sum(
                jnp.exp(scores_rows(args[0], args[1], col_pot) - args[2][:, None]), axis=1
            ),
            (row_blocks, norm_blocks, row_peaks.reshape(block_count, block_rows)),
        ).reshape(row_count)
        row_totals = lax.psum(row_totals, "col")
        row_pot = epsilon * math.log(total_data) - epsilon * (row_peaks + jnp.log(row_totals))
        pot_blocks = row_pot.reshape(block_count, block_rows)
        lowest = jnp.full((col_count,), -jnp.inf, jnp.float32)
        nothing = jnp.zeros((col_count,), jnp.float32)

        def peak_step(carry, args):
            return (
                jnp.maximum(carry, jnp.max(scores_cols(args[0], args[1], args[2]), axis=0)),
                None,
            )

        col_peaks, _ = lax.scan(peak_step, lowest, (row_blocks, norm_blocks, pot_blocks))
        col_peaks = lax.pmax(col_peaks, "row")

        def total_step(carry, args):
            scores = scores_cols(args[0], args[1], args[2])
            return (carry + jnp.sum(jnp.exp(scores - col_peaks[None, :]), axis=0), None)

        totals, _ = lax.scan(total_step, nothing, (row_blocks, norm_blocks, pot_blocks))
        totals = lax.psum(totals, "row")
        col_pot = epsilon * math.log(total_noise) - epsilon * (col_peaks + jnp.log(totals))

    def shifted_sums(rows, norms, shift):
        weights = jnp.exp(scores_rows(rows, norms, col_pot) - shift[:, None])
        denom = jnp.sum(weights, axis=1)
        numer = jnp.dot(weights, cols_all, precision=highest)
        return (denom, numer)

    peaks = lax.map(
        lambda args: jnp.max(scores_rows(args[0], args[1], col_pot), axis=1),
        (row_blocks, norm_blocks),
    ).reshape(row_count)
    peaks = lax.pmax(peaks, "col")
    denoms, numers = lax.map(
        lambda args: shifted_sums(args[0], args[1], args[2]),
        (row_blocks, norm_blocks, peaks.reshape(block_count, block_rows)),
    )
    denoms = denoms.reshape(row_count)
    numers = numers.reshape(row_count, features)
    denoms, numers = (
        lax.psum_scatter(denoms, "col", scatter_dimension=0, tiled=True),
        lax.psum_scatter(numers, "col", scatter_dimension=0, tiled=True),
    )
    targets = numers / denoms[:, None]
    path = (1.0 - times)[:, None] * noise + times[:, None] * targets
    velocity = targets - noise
    return (path, velocity)


def solution(mesh):
    in_specs = (P(("row", "col"), None), P(("col", "row"), None), P(("row", "col")))
    out_specs = (P(("row", "col"), None), P(("row", "col"), None))
    return jax.shard_map(
        per_device, mesh=mesh, in_specs=in_specs, out_specs=out_specs, check_vma=False
    )
```

profile of v0, /device:TPU:0, one launch (start us, length us, event | category | flops | bytes accessed | tf_op | source)
XLA Modules:
  0.0 399.2 jit_solution(12491608517140798521)
XLA Ops:
  7.2 0.0 all-gather.3.cloned.1.call-start
  7.2 0.7 all-gather.3.cloned.1.call-update
  7.9 0.0 all-gather.5.cloned.1.call-start
  7.9 0.7 all-gather.5.cloned.1.call-update
  8.6 0.0 reduce-scatter.2.cloned.1.call-start
  8.7 40.6 %all-gather.3.cloned.1.call-done = f32[512,2048]{1,0:T(8,128)} async-done(((f32[64,2048]{1,0:T(8,128)}), f32[512,2048]{1,0:T(8,128)}) %all-gather.3.cloned.1.call-update) | async-done | bytes 4194320 | tf_op jit(solution)/shard_map/all_gather | solution.py:21
  49.3 2.5 multiply_reduce_fusion.1
  51.9 148.7 %all-gather.5.cloned.1.call-done = f32[1024,2048]{1,0:T(8,128)} async-done(((f32[256,2048]{1,0:T(8,128)}), f32[1024,2048]{1,0:T(8,128)}) %all-gather.5.cloned.1.call-update) | async-done | bytes 8388624 | tf_op jit(solution)/shard_map/all_gather | solution.py:22
  200.6 0.0 copy-start
  200.6 4.1 %multiply_reduce_fusion = f32[1024]{0:T(1024)S(1)} fusion(f32[1024,2048]{1,0:T(8,128)} %all-gather.5.cloned.1.call-done), kind=kLoop, calls=%fused_computation | loop fusion | flops 4193280 | bytes 8392704 | tf_op jit(solution)/shard_map/reduce_sum | solution.py:31
  204.7 1.6 copy-done
  206.3 16.5 %fusion = (f32[512]{0:T(512)S(1)}, f32[512,1024]{1,0:T(8,128)S(1)}) fusion(f32[512,2048]{1,0:T(8,128)} %all-gather.3.cloned.1.call-done, f32[1024,2048]{1,0:T(8,128)S(1)} %copy-done, f32[1024]{0:T(1024)S(1)} %multiply_reduce_fusion, f32[512]{0:T(512)S(1)} %multiply_reduce_fusion.1), kind=kOutput, calls=%fused_computation.13 | convolution fusion | flops 12888571904 | bytes 14688256 | tf_op jit(solution)/shard_map/while/body/eval_jaxpr/dot_general | solution.py:16
  222.9 13.8 %pmax.35 = f32[512]{0:T(512)S(1)} all-reduce(f32[512]{0:T(512)S(1)} %get-tuple-element.156), channel_id=1, replica_groups=mesh['row'=4,'col'=8] {'col'}, use_global_device_ids=true, to_apply=%region_3.4 | all-reduce | flops 512 | bytes 4096 | tf_op jit(solution)/shard_map/pmax | solution.py:47
  236.7 0.6 exponential_reduce_fusion.3
  237.2 11.8 %psum.28 = f32[512]{0:T(512)S(1)} all-reduce(f32[512]{0:T(512)S(1)} %exponential_reduce_fusion.3), channel_id=1, replica_groups=mesh['row'=4,'col'=8] {'col'}, use_global_device_ids=true, to_apply=%region_5.6 | all-reduce | flops 512 | bytes 4096 | tf_op jit(solution)/shard_map/psum | solution.py:54
  249.1 0.3 fusion.1
  249.3 8.9 %pmax.36 = f32[1024]{0:T(1024)S(1)} all-reduce(f32[1024]{0:T(1024)S(1)} %fusion.1), channel_id=1, replica_groups=mesh['row'=4,'col'=8] {'row'}, use_global_device_ids=true, to_apply=%region_7.8 | all-reduce | flops 1024 | bytes 8192 | tf_op jit(solution)/shard_map/pmax | solution.py:67
  258.3 0.5 exponential_reduce_fusion.2
  258.8 9.9 %psum.29 = f32[1024]{0:T(1024)S(1)} all-reduce(f32[1024]{0:T(1024)S(1)} %exponential_reduce_fusion.2), channel_id=1, replica_groups=mesh['row'=4,'col'=8] {'row'}, use_global_device_ids=true, to_apply=%region_9.10 | all-reduce | flops 1024 | bytes 8192 | tf_op jit(solution)/shard_map/psum | solution.py:74
  268.7 0.3 fusion.2
  268.9 11.8 %pmax.37 = f32[512]{0:T(512)S(1)} all-reduce(f32[512]{0:T(512)S(1)} %fusion.2), channel_id=1, replica_groups=mesh['row'=4,'col'=8] {'col'}, use_global_device_ids=true, to_apply=%region_11.12 | all-reduce | flops 512 | bytes 4096 | tf_op jit(solution)/shard_map/pmax | solution.py:47
  280.7 0.6 exponential_reduce_fusion.1
  281.3 11.8 %psum.30 = f32[512]{0:T(512)S(1)} all-reduce(f32[512]{0:T(512)S(1)} %exponential_reduce_fusion.1), channel_id=1, replica_groups=mesh['row'=4,'col'=8] {'col'}, use_global_device_ids=true, to_apply=%region_13.14 | all-reduce | flops 512 | bytes 4096 | tf_op jit(solution)/shard_map/psum | solution.py:54
  293.1 0.3 fusion.3
  293.4 8.9 %pmax.38 = f32[1024]{0:T(1024)S(1)} all-reduce(f32[1024]{0:T(1024)S(1)} %fusion.3), channel_id=1, replica_groups=mesh['row'=4,'col'=8] {'row'}, use_global_device_ids=true, to_apply=%region_15.16 | all-reduce | flops 1024 | bytes 8192 | tf_op jit(solution)/shard_map/pmax | solution.py:67
  302.3 0.5 exponential_reduce_fusion
  302.8 9.9 %psum.31 = f32[1024]{0:T(1024)S(1)} all-reduce(f32[1024]{0:T(1024)S(1)} %exponential_reduce_fusion), channel_id=1, replica_groups=mesh['row'=4,'col'=8] {'row'}, use_global_device_ids=true, to_apply=%region_17.18 | all-reduce | flops 1024 | bytes 8192 | tf_op jit(solution)/shard_map/psum | solution.py:74
  312.7 0.3 fusion.4
  313.0 11.8 %pmax.39 = f32[512]{0:T(512)S(1)} all-reduce(f32[512]{0:T(512)S(1)} %fusion.4), channel_id=1, replica_groups=mesh['row'=4,'col'=8] {'col'}, use_global_device_ids=true, to_apply=%region_19.20 | all-reduce | flops 512 | bytes 4096 | tf_op jit(solution)/shard_map/pmax | solution.py:87
  324.8 17.9 %fusion.6 = f32[512,2048]{1,0:T(8,128)} fusion(f32[1024,2048]{1,0:T(8,128)} %all-gather.5.cloned.1.call-done, f32[512,1024]{1,0:T(8,128)S(1)} %get-tuple-element.157, f32[512]{0:T(512)S(1)} %pmax.39, f32[1024]{0:T(1024)S(1)} %multiply_subtract_fusion), kind=kOutput, calls=%fused_computation.19 | convolution fusion | flops 12886474752 | bytes 14686208 | tf_op jit(solution)/shard_map/while/body/eval_jaxpr/dot_general | solution.py:80
  342.7 0.0 copy-start.3
  342.7 0.0 copy-start.2
  342.7 0.0 reduce-scatter.2.cloned.1.call-update
  342.7 0.0 copy-start.1
  342.7 0.6 copy-done.3
  343.3 0.6 dynamic-slice.7
  344.6 0.0 copy-done.2
  344.6 0.6 fusion.5
  345.2 11.8 %all-reduce = f32[512]{0:T(512)S(1)} all-reduce(f32[512]{0:T(512)S(1)} %fusion.5), channel_id=3, replica_groups=mesh['row'=4,'col'=8] {'col'}, use_global_device_ids=true, to_apply=%region_22.23.clone | all-reduce | flops 512 | bytes 4096
  356.9 0.1 dynamic-slice.8
  357.0 33.5 %reduce-scatter.2.cloned.1.call-done = f32[64,2048]{1,0:T(8,128)} async-done(((f32[512,2048]{1,0:T(8,128)}), f32[64,2048]{1,0:T(8,128)}) %reduce-scatter.2.cloned.1.call-update) | async-done | bytes 524304 | tf_op jit(solution)/shard_map/reduce_scatter | solution.py:96
  390.5 0.0 copy-done.1
  390.5 2.2 fusion.10
  (5 shorter events, 0.0 us)
Async XLA Ops:
  7.2 42.2 %all-gather.3.cloned.1.call-start = ((), (), s32[]{:S(2)}) async-start(), calls=%async_computation.1 | async-start | bytes 4718592 | tf_op jit(solution)/shard_map/all_gather | solution.py:21
  7.9 192.7 %all-gather.5.cloned.1.call-start = ((), (), s32[]{:S(2)}) async-start(), calls=%async_computation.2 | async-start | bytes 10485760 | tf_op jit(solution)/shard_map/all_gather | solution.py:22
  8.6 381.9 %reduce-scatter.2.cloned.1.call-start = ((), (), s32[]{:S(2)}) async-start(), calls=%async_computation.3 | async-start | bytes 4718592 | tf_op jit(solution)/shard_map/reduce_scatter | solution.py:96
  200.6 5.8 %copy-start = (f32[1024,2048]{1,0:T(8,128)S(1)}, f32[1024,2048]{1,0:T(8,128)}, u32[]{:S(2)}) copy-start(f32[1024,2048]{1,0:T(8,128)} %all-gather.5.cloned.1.call-done) | copy-start | bytes 25165828
  342.7 0.7 copy-start.3
  342.7 1.9 copy-start.2
  342.7 47.8 %copy-start.1 = (f32[64,2048]{1,0:T(8,128)S(1)}, f32[64,2048]{1,0:T(8,128)}, u32[]{:S(2)}) copy-start(f32[64,2048]{1,0:T(8,128)} %param.3) | copy-start | bytes 1572868
Sparse Core Ops, SparseCore 0:
  9.9 39.4 all-gather.2
  50.9 149.6 all-gather.4
  342.8 47.6 reduce-scatter.1
where the time goes:
time: 400 us; the launch traced here: 399 us
  waiting for transfers between devices  224 us (56%)
  blocking collectives  110 us (28%)
  matrix products  34.4 us (9%)
  between operations  14.5 us (4%)
  other arithmetic  12.7 us (3%)
    all_gather x1, waiting for transfers between devices, per_device(): cols_all = lax.all_gather(data, 'row', axis=0, tiled=True)  149 us
    all_gather x1, waiting for transfers between devices, per_device(): rows_all = lax.all_gather(noise, 'col', axis=0, tiled=True)  40.6 us
    reduce_scatter x1, waiting for transfers between devices, per_device(): lax.psum_scatter(numers, 'col', scatter_dimension=0, tiled=True)  33.5 us
    pmax x2, blocking collectives, per_device(): row_peaks = lax.pmax(row_peaks, 'col')  25.6 us
    psum x2, blocking collectives, per_device(): row_totals = lax.psum(row_totals, 'col')  23.6 us
    psum x2, blocking collectives, per_device(): totals = lax.psum(totals, 'row')  19.8 us
    dot_general x1, matrix products, shifted_sums(): numer = jnp.dot(weights, cols_all, precision=highest)  17.9 us
    pmax x2, blocking collectives, per_device(): col_peaks = lax.pmax(col_peaks, 'row')  17.8 us
  transfers between devices with their start and end apart: 3, of which 3 were waited for; matrix products, arithmetic and copies ran while one was open for 1% of the time, Pallas kernels for 0%

commit v1 on v0

v1 whole, which is shorter than its diff:
```python
import functools
import math

import jax
import jax.numpy as jnp
from jax import lax
from jax.experimental import pallas as pl
from jax.experimental.pallas import tpu as pltpu
from jax.sharding import PartitionSpec as P

ITERS = 2
EPS = 0.05
PAIR = 2
CORES = 2
QUAD = PAIR * CORES
PIECES = 4
f32 = jnp.float32
bf16 = jnp.bfloat16
NT = (((1,), (1,)), ((), ()))
NN = (((1,), (0,)), ((), ()))


def split(value):
    high = value.astype(bf16)
    return high, (value - high.astype(f32)).astype(bf16)


def dot3(ah, al, bh, bl, dims):
    mm = functools.partial(lax.dot_general, dimension_numbers=dims, preferred_element_type=f32)
    return mm(ah, bh) + (mm(al, bh) + mm(ah, bl))


def kernel(
    Z, Y, noise_ref, data_ref, out_ref,
    nf, df, nh, nl, dh, dl, rn, cn, score, st, wh, wl, rs, cs, part, yb, ub, db,
    up_s, up_r, dn_s, dn_r, ys, yr, xs, xr, sib, fs, fr, rss, rsr, css, csr,
    ps, pr, us, ur, vs, vr,
):
    nb, D = noise_ref.shape
    md = data_ref.shape[0]
    G = Z * Y
    R, C = G * nb, QUAD * md
    mc = md // PIECES
    total_noise, total_data = R * QUAD, C * G
    z = lax.axis_index("row")
    col = lax.axis_index("col")
    c = lax.rem(col, CORES)
    x = lax.rem(lax.div(col, CORES), PAIR)
    y = lax.div(col, QUAD)
    g = z * Y + y
    q = x * CORES + c

    def dev(z_, y_, x_, c_):
        return (z_, (y_ * PAIR + x_) * CORES + c_)

    def rc(src, dst, send, recv, device):
        return pltpu.make_async_remote_copy(
            src_ref=src, dst_ref=dst, send_sem=send, recv_sem=recv,
            device_id=device, device_id_type=pl.DeviceIdType.MESH,
        )

    def group_dev(g2):
        return dev(lax.div(g2, Y), lax.rem(g2, Y), x, c)

    def quad_dev(q2):
        return dev(z, y, lax.div(q2, CORES), lax.rem(q2, CORES))

    barrier = pltpu.get_barrier_semaphore()
    for r in range(1, G):
        pl.semaphore_signal(barrier, inc=1, device_id=group_dev(lax.rem(g + r, G)),
                            device_id_type=pl.DeviceIdType.MESH)
    for r in range(1, QUAD):
        pl.semaphore_signal(barrier, inc=1, device_id=quad_dev(lax.rem(q + r, QUAD)),
                            device_id_type=pl.DeviceIdType.MESH)
    pl.semaphore_wait(barrier, G - 1 + QUAD - 1)

    x_dev = dev(z, y, 1 - x, c)
    c_dev = dev(z, y, x, 1 - c)
    qx = (1 - x) * CORES + c
    qc = x * CORES + 1 - c
    qxc = (1 - x) * CORES + 1 - c

    def data_send(k):
        rows = pl.ds(k * mc, mc)
        return rc(data_ref.at[rows], df.at[q, rows], xs.at[k], xr.at[k], x_dev)

    def data_recv(k):
        rows = pl.ds(k * mc, mc)
        return rc(data_ref.at[rows], df.at[qx, rows], xs.at[k], xr.at[k], x_dev)

    def data_forward(k):
        rows = pl.ds(k * mc, mc)
        return rc(df.at[qx, rows], df.at[qx, rows], fs.at[k], fr.at[k], c_dev)

    def data_forwarded(k):
        rows = pl.ds(k * mc, mc)
        return rc(df.at[qxc, rows], df.at[qxc, rows], fs.at[k], fr.at[k], c_dev)

    def up_copy(zz, s):
        slot = nf.at[zz * Y + y]
        return rc(slot, slot, up_s.at[s], up_r.at[s], dev(z + 1, y, x, c))

    def dn_copy(zz, s):
        slot = nf.at[zz * Y + y]
        return rc(slot, slot, dn_s.at[s], dn_r.at[s], dev(z - 1, y, x, c))

    def y_copy(zz, r):
        slot = nf.at[zz * Y + y]
        return rc(slot, slot, ys.at[zz, r], yr.at[zz, y], dev(z, lax.rem(y + r, Y), x, c))

    def y_landed(zz, r):
        y2 = lax.rem(y + r, Y)
        slot = nf.at[zz * Y + y2]
        return rc(slot, slot, ys.at[zz, r], yr.at[zz, y2], dev(z, y2, x, c))

    def y_sends(zz):
        for r in range(1, Y):
            y_copy(zz, r).start()

    for k in range(PIECES):
        data_send(k).start()
    sib_copy = rc(data_ref, df.at[q], sib.at[0], sib.at[1], c_dev)
    sib_copy.start()
    nf[g] = noise_ref[...]
    y_sends(z)
    pl.when(z + 1 < Z)(lambda: up_copy(z, 0).start())
    pl.when(z > 0)(lambda: dn_copy(z, 0).start())
    df[q] = data_ref[...]

    def convert(src, slot, base, at, count, high, low, norm):
        step = 16

        def body(i, carry):
            value = src[slot, pl.ds(pl.multiple_of(base + i * step, step), step), :]
            rows = pl.ds(pl.multiple_of(at + i * step, step), step)
            h, l = split(value)
            high[rows, :] = h
            low[rows, :] = l
            norm[rows, :] = jnp.broadcast_to(
                jnp.sum(value * value, axis=1, keepdims=True), (step, 128))
            return carry

        lax.fori_loop(0, count // step, body, 0)

    def convert_noise(slot):
        convert(nf, slot, 0, slot * nb, nb, nh, nl, rn)

    def convert_data(slot, k, count):
        convert(df, slot, k * mc, slot * md + k * mc, count, dh, dl, cn)

    convert_noise(g)
    convert_data(q, 0, md)
    rc(data_ref, df.at[qc], sib.at[0], sib.at[1], c_dev).wait_recv()
    convert_data(qc, 0, md)

    def y_arrivals(zz):
        for r in range(1, Y):
            y_landed(zz, r).wait_recv()
            convert_noise(zz * Y + lax.rem(y + r, Y))

    for s in range(1, Z):
        lo, hi = z - s, z + s

        @pl.when(lo >= 0)
        def _():
            up_copy(lo, s - 1).wait_recv()
            if s < Z - 1:
                pl.when(z + 1 < Z)(lambda: up_copy(lo, s).start())
            y_sends(lo)

        @pl.when(hi < Z)
        def _():
            dn_copy(hi, s - 1).wait_recv()
            if s < Z - 1:
                pl.when(z > 0)(lambda: dn_copy(hi, s).start())
            y_sends(hi)

        if s <= PIECES:
            data_recv(s - 1).wait_recv()
            data_forward(s - 1).start()

        pl.when(lo >= 0)(lambda: convert_noise(lo * Y + y))
        pl.when(hi < Z)(lambda: convert_noise(hi * Y + y))
        if s == 1:
            y_arrivals(z)
        else:
            pl.when(lo + 1 >= 0)(lambda: y_arrivals(lo + 1))
            pl.when(hi - 1 < Z)(lambda: y_arrivals(hi - 1))
        if s <= PIECES:
            convert_data(qx, s - 1, mc)
            data_forwarded(s - 1).wait_recv()
            convert_data(qxc, s - 1, mc)
    for k in range(Z - 1, PIECES):
        data_recv(k).wait_recv()
        data_forward(k).start()
        convert_data(qx, k, mc)
    pl.when(z - Z + 1 >= 0)(lambda: y_arrivals(z - Z + 1))
    pl.when(z + Z - 1 < Z)(lambda: y_arrivals(z + Z - 1))
    for k in range(Z - 1, PIECES):
        data_forwarded(k).wait_recv()
        convert_data(qxc, k, mc)

    wide = cn.shape[0] // QUAD

    def score_body(i, carry):
        rows = pl.ds(pl.multiple_of(i * wide, wide), wide)
        cross = dot3(nh[...], nl[...], dh[rows, :], dl[rows, :], NT)
        norms = cn[rows, :].T[0:1, :]
        for t in range(wide // 128):
            lanes = slice(t * 128, (t + 1) * 128)
            score[i, :, lanes] = (
                2.0 * cross[:, lanes] - rn[...] - norms[:, lanes]) * (1.0 / (D * EPS))
        return carry

    lax.fori_loop(0, QUAD, score_body, 0)

    lane = lax.broadcasted_iota(jnp.int32, (1, 128), 1)
    sub = lax.broadcasted_iota(jnp.int32, (8, 1), 0)
    block = 32

    def row_pass(pot, weights):
        def body(i, carry):
            rows = pl.ds(pl.multiple_of(i * block, block), block)
            vals = [score[j, rows, :] + (0.0 if pot is None else pot[:, j * md:(j + 1) * md])
                    for j in range(QUAD)]
            peak = functools.reduce(jnp.maximum, vals)
            peak = jnp.max(peak, axis=1, keepdims=True)
            exps = [jnp.exp(v - peak) for v in vals]
            total = jnp.sum(functools.reduce(jnp.add, exps), axis=1, keepdims=True)
            st[rows, :] = jnp.where(lane == 0, peak, total)
            if weights:
                for j in range(QUAD):
                    h, l = split(exps[j])
                    wh[rows, j * md:(j + 1) * md] = h
                    wl[rows, j * md:(j + 1) * md] = l
            return carry

        lax.fori_loop(0, R // block, body, 0)

    def row_copy(ex, r, landed=False):
        g2 = lax.rem(g + r, G)
        at = g2 if landed else g
        return rc(rs.at[ex, at], rs.at[ex, at], rss.at[ex, r], rsr.at[ex, at], group_dev(g2))

    def row_exchange(ex):
        rs[ex, g] = st[...].T[0:8, :]
        for r in range(1, G):
            row_copy(ex, r).start()

    def row_combine(ex):
        for r in range(1, G):
            row_copy(ex, r, True).wait_recv()
        peaks = [rs[ex, k][0:1, :] for k in range(G)]
        top = functools.reduce(jnp.maximum, peaks)
        total = sum(rs[ex, k][1:2, :] * jnp.exp(peaks[k] - top) for k in range(G))
        return top, total

    def col_copy(ex, r, landed=False):
        q2 = lax.rem(q + r, QUAD)
        at = q2 if landed else q
        return rc(cs.at[ex, at], cs.at[ex, at], css.at[ex, r], csr.at[ex, at], quad_dev(q2))

    def spread(row):
        return jnp.broadcast_to(row, (128, row.shape[1])).T

    pot = None
    for step in range(ITERS):
        row_pass(pot, False)
        row_exchange(step)
        top, total = row_combine(step)
        st[...] = spread(math.log(total_data) - (top + jnp.log(total)))
        for j in range(QUAD):
            for t in range(md // 128):
                lanes = slice(t * 128, (t + 1) * 128)
                val = score[j, :, lanes] + st[...]
                peak = jnp.max(val, axis=0, keepdims=True)
                total = jnp.sum(jnp.exp(val - peak), axis=0, keepdims=True)
                cs[step, q, :, j * md + t * 128:j * md + (t + 1) * 128] = jnp.where(
                    sub == 0, peak, total)
        for r in range(1, QUAD):
            col_copy(step, r).start()
        for r in range(1, QUAD):
            col_copy(step, r, True).wait_recv()
        peaks = [cs[step, k][0:1, :] for k in range(QUAD)]
        top = functools.reduce(jnp.maximum, peaks)
        total = sum(cs[step, k][1:2, :] * jnp.exp(peaks[k] - top) for k in range(QUAD))
        pot = math.log(total_noise) - (top + jnp.log(total))

    row_pass(pot, True)
    row_exchange(ITERS)
    mine = st[...].T[0:1, :]
    top, total = row_combine(ITERS)
    st[...] = spread(jnp.exp(mine - top) / total)

    def order(i):
        d = Z - 1 - lax.div(i, 2)
        return jnp.where(lax.rem(i, 2) == 0, z + d, z - d)

    def part_copy(zz, r):
        y2 = lax.rem(y + r, Y)
        return rc(part.at[zz, y2], yb.at[zz, y], ps.at[zz, r], pr.at[zz, y], dev(z, y2, x, c))

    def part_landed(zz, r):
        y2 = lax.rem(y + r, Y)
        return rc(part.at[zz, y2], yb.at[zz, y2], ps.at[zz, r], pr.at[zz, y2], dev(z, y2, x, c))

    def up_part(zz):
        return rc(part.at[zz, y], ub.at[zz], us.at[zz], ur.at[zz], dev(z + 1, y, x, c))

    def dn_part(zz):
        return rc(part.at[zz, y], db.at[zz], vs.at[zz], vr.at[zz], dev(z - 1, y, x, c))

    def partial_body(i, carry):
        zz = order(i)

        @pl.when((zz >= 0) & (zz < Z))
        def _():
            rows = pl.ds(pl.multiple_of(zz * (Y * nb), Y * nb), Y * nb)
            ah, al = wh[rows, :], wl[rows, :]
            scale = st[rows, :]
            for n in range(D // 256):
                lanes = slice(n * 256, (n + 1) * 256)
                numer = dot3(ah, al, dh[:, lanes], dl[:, lanes], NN)
                for t in range(2):
                    piece = numer[:, t * 128:(t + 1) * 128] * scale
                    for k in range(Y):
                        part[zz, k, :, n * 256 + t * 128:n * 256 + (t + 1) * 128] = (
                            piece[k * nb:(k + 1) * nb])
            for r in range(1, Y):
                part_copy(zz, r).start()

        return carry

    lax.fori_loop(0, 2 * Z - 1, partial_body, 0)

    def reduce_body(i, carry):
        zz = order(i)

        @pl.when((zz >= 0) & (zz < Z))
        def _():
            for r in range(1, Y):
                part_landed(zz, r).wait_recv()
                part[zz, y] += yb[zz, lax.rem(y + r, Y)]

            @pl.when((zz >= z) & (z > 0))
            def _():
                up_part(zz).wait_recv()
                part[zz, y] += ub[zz]

            @pl.when((zz <= z) & (z + 1 < Z))
            def _():
                dn_part(zz).wait_recv()
                part[zz, y] += db[zz]

            pl.when(zz > z)(lambda: up_part(zz).start())
            pl.when(zz < z)(lambda: dn_part(zz).start())

        return carry

    lax.fori_loop(0, 2 * Z - 1, reduce_body, 0)
    out_ref[...] = part[z, y]

    for k in range(PIECES):
        data_send(k).wait_send()
        data_forward(k).wait_send()
    sib_copy.wait_send()
    for s in range(Z - 1):
        pl.when((z - s >= 0) & (z + 1 < Z))(lambda: up_copy(z - s, s).wait_send())
        pl.when((z + s < Z) & (z > 0))(lambda: dn_copy(z + s, s).wait_send())
    for ex in range(ITERS + 1):
        for r in range(1, G):
            row_copy(ex, r).wait_send()
    for ex in range(ITERS):
        for r in range(1, QUAD):
            col_copy(ex, r).wait_send()
    for zz in range(Z):
        for r in range(1, Y):
            y_copy(zz, r).wait_send()
            part_copy(zz, r).wait_send()
        pl.when(zz > z)(lambda: up_part(zz).wait_send())
        pl.when(zz < z)(lambda: dn_part(zz).wait_send())


def targets_of(Z, Y, noise, data):
    nb, D = noise.shape
    md = data.shape[0]
    G = Z * Y
    R, C = G * nb, QUAD * md
    V, dma = pltpu.VMEM, pltpu.SemaphoreType.DMA
    flops = 2 * 6 * R * C * D
    return pl.pallas_call(
        functools.partial(kernel, Z, Y),
        out_shape=jax.ShapeDtypeStruct((nb, D), f32),
        in_specs=[pl.BlockSpec(memory_space=pltpu.VMEM)] * 2,
        out_specs=pl.BlockSpec(memory_space=pltpu.VMEM),
        scratch_shapes=[
            V((G, nb, D), f32), V((QUAD, md, D), f32),
            V((R, D), bf16), V((R, D), bf16), V((C, D), bf16), V((C, D), bf16),
            V((R, 128), f32), V((C, 128), f32),
            V((QUAD, R, md), f32), V((R, 128), f32),
            V((R, C), bf16), V((R, C), bf16),
            V((ITERS + 1, G, 8, R), f32), V((ITERS, QUAD, 8, C), f32),
            V((Z, Y, nb, D), f32), V((Z, Y, nb, D), f32), V((Z, nb, D), f32), V((Z, nb, D), f32),
            dma((Z,)), dma((Z,)), dma((Z,)), dma((Z,)),
            dma((Z, Y)), dma((Z, Y)),
            dma((PIECES,)), dma((PIECES,)), dma((2,)), dma((PIECES,)), dma((PIECES,)),
            dma((ITERS + 1, G)), dma((ITERS + 1, G)), dma((ITERS, QUAD)), dma((ITERS, QUAD)),
            dma((Z, Y)), dma((Z, Y)), dma((Z,)), dma((Z,)), dma((Z,)), dma((Z,)),
        ],
        compiler_params=pltpu.CompilerParams(
            collective_id=0, has_side_effects=True, vmem_limit_bytes=60 * 1024 * 1024),
        cost_estimate=pl.CostEstimate(
            flops=flops, bytes_accessed=8 * (R + C) * D, transcendentals=5 * R * C),
    )(noise, data)


def per_device(Z, Y, noise, data, times):
    targets = targets_of(Z, Y, noise, data)
    path = (1.0 - times)[:, None] * noise + times[:, None] * targets
    return (path, targets - noise)


def solution(mesh):
    Z, Y = mesh.shape["row"], mesh.shape["col"] // QUAD
    in_specs = (P(("row", "col"), None), P(("col", "row"), None), P(("row", "col")))
    out_specs = (P(("row", "col"), None), P(("row", "col"), None))
    return jax.shard_map(
        functools.partial(per_device, Z, Y), mesh=mesh, in_specs=in_specs, out_specs=out_specs,
        check_vma=False,
    )
```

time: 400 us -> 152 us (0.38)
  waiting for transfers between devices: 224 us -> 0 us
  Pallas kernels: 0 us -> 149 us
  blocking collectives: 110 us -> 0 us
  matrix products: 34.4 us -> 0 us
  between operations: 14.5 us -> 0.65 us
  other arithmetic: 12.7 us -> 2.73 us
    all_gather x2 -> x0, waiting for transfers between devices: 189 us -> none  [the longest x1 149 us: per_device(): cols_all = lax.all_gather(data, 'row', axis=0, tiled=True)]
    pallas_call x0 -> x1, Pallas kernels: none -> 149 us  [targets_of(): pl.pallas_call(functools.partial(kernel, Z, Y), out_shape=jax.ShapeDtypeS...]
    pmax x5 -> x0, blocking collectives: 55.2 us -> none  [the longest x2 25.6 us: per_device(): row_peaks = lax.pmax(row_peaks, 'col')]
    psum x4 -> x0, blocking collectives: 43.4 us -> none  [the longest x2 23.6 us: per_device(): row_totals = lax.psum(row_totals, 'col')]
    dot_general x2 -> x0, matrix products: 34.4 us -> none  [the longest x1 17.9 us: shifted_sums(): numer = jnp.dot(weights, cols_all, precision=highest)]
    reduce_scatter x1 -> x0, waiting for transfers between devices: 33.5 us -> none  [per_device(): lax.psum_scatter(numers, 'col', scatter_dimension=0, tiled=True)]
    unnamed x1 -> x0, blocking collectives: 11.8 us -> none
    reduce_sum x7 -> x0, other arithmetic: 9.35 us -> none  [the longest x1 4.15 us: per_device(): col_norms = jnp.sum(cols_all * cols_all, axis=1)]
  transfers between devices with their start and end apart: 3 -> 0, of which waited for: 3 -> 0; matrix products, arithmetic and copies ran while one was open for 1% -> 0% of each run, Pallas kernels for 0% -> 0%
where the time goes in v1:
time: 152 us
  Pallas kernels  149 us (98%)
  other arithmetic  2.73 us (2%)
    pallas_call x1, Pallas kernels, targets_of(): pl.pallas_call(functools.partial(kernel, Z, Y), out_shape=jax.ShapeDtypeS...  149 us

profile of v1, /device:TPU:0, one launch (start us, length us, event | category | flops | bytes accessed | tf_op | source)
XLA Modules:
  0.0 152.0 jit_solution(3214714619267692946)
XLA Ops:
  0.6 0.7 broadcast_subtract_fusion
  1.3 0.0 copy-start
  1.3 0.0 copy-start.1
  1.3 148.6 %shard_map.50 = f32[64,2048]{1,0:T(8,128)} custom-call(f32[64,2048]{1,0:T(8,128)} %noise_ref.1, f32[256,2048]{1,0:T(8,128)} %data_ref.1), custom_call_target="tpu_custom_call" | custom-call | flops 12884901888 | bytes 25165824 | tf_op jit(solution)/shard_map/pallas_call | solution.py:391
  149.9 0.0 copy-done
  149.9 0.0 copy-done.1
  150.0 2.1 %fusion = (f32[64,2048]{1,0:T(8,128)}, f32[64,2048]{1,0:T(8,128)}) fusion(f32[64,2048]{1,0:T(8,128)} %shard_map.50, f32[64,2048]{1,0:T(8,128)S(1)} %copy-done, f32[64]{0:T(128)S(1)} %copy-done.1, f32[64]{0:T(128)S(1)} %broadcast_subtract_fusion), kind=kLoop, calls=%fused_computation.2 | loop fusion | flops 524288 | bytes 2097664 | tf_op jit(solution)/shard_map/sub | solution.py:420
Async XLA Ops:
  1.3 148.6 %copy-start = (f32[64,2048]{1,0:T(8,128)S(1)}, f32[64,2048]{1,0:T(8,128)}, u32[]{:S(2)}) copy-start(f32[64,2048]{1,0:T(8,128)} %noise_ref.1) | copy-start | bytes 1572868
  1.3 148.7 %copy-start.1 = (f32[64]{0:T(128)S(1)}, f32[64]{0:T(128)}, u32[]{:S(2)}) copy-start(f32[64]{0:T(128)} %param.5) | copy-start | bytes 772

commit v2 on v1

--- a/solution.py
+++ b/solution.py
@@ -14,6 +14,7 @@
 CORES = 2
 QUAD = PAIR * CORES
 PIECES = 4
+AHEAD = 2
 f32 = jnp.float32
 bf16 = jnp.bfloat16
 NT = (((1,), (1,)), ((), ()))
@@ -28,6 +29,13 @@
 def dot3(ah, al, bh, bl, dims):
     mm = functools.partial(lax.dot_general, dimension_numbers=dims, preferred_element_type=f32)
     return mm(ah, bh) + (mm(al, bh) + mm(ah, bl))
+
+
+def dot3_stacked(both, bh, bl, dims):
+    mm = functools.partial(lax.dot_general, dimension_numbers=dims, preferred_element_type=f32)
+    n = both.shape[0] // 2
+    pair = mm(both, bh)
+    return pair[:n] + (pair[n:] + mm(both[:n], bl))
 
 
 def kernel(
@@ -117,7 +125,7 @@
         for r in range(1, Y):
             y_copy(zz, r).start()
 
-    for k in range(PIECES):
+    for k in range(AHEAD):
         data_send(k).start()
     sib_copy = rc(data_ref, df.at[q], sib.at[0], sib.at[1], c_dev)
     sib_copy.start()
@@ -128,7 +136,7 @@
     df[q] = data_ref[...]
 
     def convert(src, slot, base, at, count, high, low, norm):
-        step = 16
+        step = min(32, count)
 
         def body(i, carry):
             value = src[slot, pl.ds(pl.multiple_of(base + i * step, step), step), :]
@@ -178,6 +186,8 @@
         if s <= PIECES:
             data_recv(s - 1).wait_recv()
             data_forward(s - 1).start()
+            if s - 1 + AHEAD < PIECES:
+                data_send(s - 1 + AHEAD).start()
 
         pl.when(lo >= 0)(lambda: convert_noise(lo * Y + y))
         pl.when(hi < Z)(lambda: convert_noise(hi * Y + y))
@@ -193,6 +203,8 @@
     for k in range(Z - 1, PIECES):
         data_recv(k).wait_recv()
         data_forward(k).start()
+        if k + AHEAD < PIECES:
+            data_send(k + AHEAD).start()
         convert_data(qx, k, mc)
     pl.when(z - Z + 1 >= 0)(lambda: y_arrivals(z - Z + 1))
     pl.when(z + Z - 1 < Z)(lambda: y_arrivals(z + Z - 1))
@@ -216,7 +228,7 @@
 
     lane = lax.broadcasted_iota(jnp.int32, (1, 128), 1)
     sub = lax.broadcasted_iota(jnp.int32, (8, 1), 0)
-    block = 32
+    block = 128
 
     def row_pass(pot, weights):
         def body(i, carry):
@@ -292,9 +304,14 @@
     top, total = row_combine(ITERS)
     st[...] = spread(jnp.exp(mine - top) / total)
 
-    def order(i):
-        d = Z - 1 - lax.div(i, 2)
-        return jnp.where(lax.rem(i, 2) == 0, z + d, z - d)
+    far, near = jnp.maximum(z, Z - 1 - z), jnp.minimum(z, Z - 1 - z)
+    toward = jnp.where(Z - 1 - z >= z, 1, -1)
+
+    def order(n):
+        m = n - (far - near)
+        late = near - lax.div(jnp.maximum(m, 0), 2)
+        flip = jnp.where(lax.rem(jnp.maximum(m, 0), 2) == 0, 1, -1)
+        return z + toward * jnp.where(m < 0, far - n, late * flip)
 
     def part_copy(zz, r):
         y2 = lax.rem(y + r, Y)
@@ -310,54 +327,55 @@
     def dn_part(zz):
         return rc(part.at[zz, y], db.at[zz], vs.at[zz], vr.at[zz], dev(z - 1, y, x, c))
 
-    def partial_body(i, carry):
-        zz = order(i)
-
-        @pl.when((zz >= 0) & (zz < Z))
-        def _():
-            rows = pl.ds(pl.multiple_of(zz * (Y * nb), Y * nb), Y * nb)
-            ah, al = wh[rows, :], wl[rows, :]
-            scale = st[rows, :]
-            for n in range(D // 256):
-                lanes = slice(n * 256, (n + 1) * 256)
-                numer = dot3(ah, al, dh[:, lanes], dl[:, lanes], NN)
-                for t in range(2):
-                    piece = numer[:, t * 128:(t + 1) * 128] * scale
-                    for k in range(Y):
-                        part[zz, k, :, n * 256 + t * 128:n * 256 + (t + 1) * 128] = (
-                            piece[k * nb:(k + 1) * nb])
+    def multiply(zz):
+        rows = pl.ds(pl.multiple_of(zz * (Y * nb), Y * nb), Y * nb)
+        both = jnp.concatenate([wh[rows, :], wl[rows, :]], axis=0)
+        scale = st[rows, :]
+        for n in range(D // 256):
+            lanes = slice(n * 256, (n + 1) * 256)
+            numer = dot3_stacked(both, dh[:, lanes], dl[:, lanes], NN)
+            for t in range(2):
+                piece = numer[:, t * 128:(t + 1) * 128] * scale
+                for k in range(Y):
+                    part[zz, k, :, n * 256 + t * 128:n * 256 + (t + 1) * 128] = (
+                        piece[k * nb:(k + 1) * nb])
+
+    def reduce_step(zz):
+        for r in range(1, Y):
+            part[zz, y] += yb[zz, lax.rem(y + r, Y)]
+
+        @pl.when((zz >= z) & (z > 0))
+        def _():
+            up_part(zz).wait_recv()
+            part[zz, y] += ub[zz]
+
+        @pl.when((zz <= z) & (z + 1 < Z))
+        def _():
+            dn_part(zz).wait_recv()
+            part[zz, y] += db[zz]
+
+        pl.when(zz > z)(lambda: up_part(zz).start())
+        pl.when(zz < z)(lambda: dn_part(zz).start())
+
+    def reduce_body(n, carry):
+        zz, last = order(n), order(n - 1)
+        pl.when(n < Z)(lambda: multiply(zz))
+
+        @pl.when(n > 0)
+        def _():
+            for r in range(1, Y):
+                part_copy(last, r).wait_send()
+                part_landed(last, r).wait_recv()
+
+        @pl.when(n < Z)
+        def _():
             for r in range(1, Y):
                 part_copy(zz, r).start()
 
+        pl.when(n > 0)(lambda: reduce_step(last))
         return carry
 
-    lax.fori_loop(0, 2 * Z - 1, partial_body, 0)
-
-    def reduce_body(i, carry):
-        zz = order(i)
-
-        @pl.when((zz >= 0) & (zz < Z))
-        def _():
-            for r in range(1, Y):
-                part_landed(zz, r).wait_recv()
-                part[zz, y] += yb[zz, lax.rem(y + r, Y)]
-
-            @pl.when((zz >= z) & (z > 0))
-            def _():
-                up_part(zz).wait_recv()
-                part[zz, y] += ub[zz]
-
-            @pl.when((zz <= z) & (z + 1 < Z))
-            def _():
-                dn_part(zz).wait_recv()
-                part[zz, y] += db[zz]
-
-            pl.when(zz > z)(lambda: up_part(zz).start())
-            pl.when(zz < z)(lambda: dn_part(zz).start())
-
-        return carry
-
-    lax.fori_loop(0, 2 * Z - 1, reduce_body, 0)
+    lax.fori_loop(0, Z + 1, reduce_body, 0)
     out_ref[...] = part[z, y]
 
     for k in range(PIECES):
@@ -376,7 +394,6 @@
     for zz in range(Z):
         for r in range(1, Y):
             y_copy(zz, r).wait_send()
-            part_copy(zz, r).wait_send()
         pl.when(zz > z)(lambda: up_part(zz).wait_send())
         pl.when(zz < z)(lambda: dn_part(zz).wait_send())
 

time: 152 us -> 146 us (0.961)
  Pallas kernels: 149 us -> 143 us
    pallas_call x1, Pallas kernels: 149 us -> 143 us  [targets_of(): pl.pallas_call(functools.partial(kernel, Z, Y), out_shape=jax.ShapeDtypeS...]
where the time goes in v2:
time: 146 us
  Pallas kernels  143 us (98%)
  other arithmetic  2.73 us (2%)
    pallas_call x1, Pallas kernels, targets_of(): pl.pallas_call(functools.partial(kernel, Z, Y), out_shape=jax.ShapeDtypeS...  143 us

profile of v2, /device:TPU:0, one launch (start us, length us, event | category | flops | bytes accessed | tf_op | source)
XLA Modules:
  0.0 146.0 jit_solution(10099535667219251065)
XLA Ops:
  0.6 0.7 broadcast_subtract_fusion
  1.3 0.0 copy-start
  1.3 0.0 copy-start.1
  1.3 142.6 %shard_map.50 = f32[64,2048]{1,0:T(8,128)} custom-call(f32[64,2048]{1,0:T(8,128)} %noise_ref.1, f32[256,2048]{1,0:T(8,128)} %data_ref.1), custom_call_target="tpu_custom_call" | custom-call | flops 12884901888 | bytes 25165824 | tf_op jit(solution)/shard_map/pallas_call | solution.py:408
  143.9 0.0 copy-done
  143.9 0.0 copy-done.1
  143.9 2.1 %fusion = (f32[64,2048]{1,0:T(8,128)}, f32[64,2048]{1,0:T(8,128)}) fusion(f32[64,2048]{1,0:T(8,128)} %shard_map.50, f32[64,2048]{1,0:T(8,128)S(1)} %copy-done, f32[64]{0:T(128)S(1)} %copy-done.1, f32[64]{0:T(128)S(1)} %broadcast_subtract_fusion), kind=kLoop, calls=%fused_computation.2 | loop fusion | flops 524288 | bytes 2097664 | tf_op jit(solution)/shard_map/sub | solution.py:437
Async XLA Ops:
  1.3 142.6 %copy-start = (f32[64,2048]{1,0:T(8,128)S(1)}, f32[64,2048]{1,0:T(8,128)}, u32[]{:S(2)}) copy-start(f32[64,2048]{1,0:T(8,128)} %noise_ref.1) | copy-start | bytes 1572868
  1.3 142.6 %copy-start.1 = (f32[64]{0:T(128)S(1)}, f32[64]{0:T(128)}, u32[]{:S(2)}) copy-start(f32[64]{0:T(128)} %param.5) | copy-start | bytes 772

commit v3 on v2

--- a/solution.py
+++ b/solution.py
@@ -14,7 +14,7 @@
 CORES = 2
 QUAD = PAIR * CORES
 PIECES = 4
-AHEAD = 2
+HALVES = 2
 f32 = jnp.float32
 bf16 = jnp.bfloat16
 NT = (((1,), (1,)), ((), ()))
@@ -125,7 +125,7 @@
         for r in range(1, Y):
             y_copy(zz, r).start()
 
-    for k in range(AHEAD):
+    for k in range(PIECES - 1):
         data_send(k).start()
     sib_copy = rc(data_ref, df.at[q], sib.at[0], sib.at[1], c_dev)
     sib_copy.start()
@@ -161,10 +161,35 @@
     rc(data_ref, df.at[qc], sib.at[0], sib.at[1], c_dev).wait_recv()
     convert_data(qc, 0, md)
 
+    def score_block(at, count, j):
+        rows, cols = pl.ds(at, count), pl.ds(pl.multiple_of(j * md, md), md)
+        both = jnp.concatenate([nh[rows, :], nl[rows, :]], axis=0)
+        cross = dot3_stacked(both, dh[cols, :], dl[cols, :], NT)
+        norms = cn[cols, :].T[0:1, :]
+        for t in range(md // 128):
+            lanes = slice(t * 128, (t + 1) * 128)
+            score[j, rows, lanes] = (
+                2.0 * cross[:, lanes] - rn[rows, :] - norms[:, lanes]) * (1.0 / (D * EPS))
+
     def y_arrivals(zz):
         for r in range(1, Y):
             y_landed(zz, r).wait_recv()
             convert_noise(zz * Y + lax.rem(y + r, Y))
+
+        def body(i, carry):
+            score_block(pl.multiple_of(zz * (Y * nb), Y * nb), Y * nb, x * CORES + i)
+            return carry
+
+        lax.fori_loop(0, CORES, body, 0)
+
+    def data_piece(k):
+        data_recv(k).wait_recv()
+        data_forward(k).start()
+        convert_data(qx, k, mc)
+
+    def data_piece_forwarded(k):
+        data_forwarded(k).wait_recv()
+        convert_data(qxc, k, mc)
 
     for s in range(1, Z):
         lo, hi = z - s, z + s
@@ -183,57 +208,49 @@
                 pl.when(z > 0)(lambda: dn_copy(hi, s).start())
             y_sends(hi)
 
-        if s <= PIECES:
-            data_recv(s - 1).wait_recv()
-            data_forward(s - 1).start()
-            if s - 1 + AHEAD < PIECES:
-                data_send(s - 1 + AHEAD).start()
-
+        if s == min(2, Z - 1):
+            data_send(PIECES - 1).start()
         pl.when(lo >= 0)(lambda: convert_noise(lo * Y + y))
         pl.when(hi < Z)(lambda: convert_noise(hi * Y + y))
+        if s == Z - 1:
+            for k in range(PIECES - 1):
+                data_piece(k)
+            for k in range(PIECES - 1):
+                data_piece_forwarded(k)
         if s == 1:
             y_arrivals(z)
         else:
             pl.when(lo + 1 >= 0)(lambda: y_arrivals(lo + 1))
             pl.when(hi - 1 < Z)(lambda: y_arrivals(hi - 1))
-        if s <= PIECES:
-            convert_data(qx, s - 1, mc)
-            data_forwarded(s - 1).wait_recv()
-            convert_data(qxc, s - 1, mc)
-    for k in range(Z - 1, PIECES):
-        data_recv(k).wait_recv()
-        data_forward(k).start()
-        if k + AHEAD < PIECES:
-            data_send(k + AHEAD).start()
-        convert_data(qx, k, mc)
     pl.when(z - Z + 1 >= 0)(lambda: y_arrivals(z - Z + 1))
     pl.when(z + Z - 1 < Z)(lambda: y_arrivals(z + Z - 1))
-    for k in range(Z - 1, PIECES):
-        data_forwarded(k).wait_recv()
-        convert_data(qxc, k, mc)
-
-    wide = cn.shape[0] // QUAD
+    data_piece(PIECES - 1)
+    data_piece_forwarded(PIECES - 1)
 
     def score_body(i, carry):
-        rows = pl.ds(pl.multiple_of(i * wide, wide), wide)
-        cross = dot3(nh[...], nl[...], dh[rows, :], dl[rows, :], NT)
-        norms = cn[rows, :].T[0:1, :]
-        for t in range(wide // 128):
+        j = (1 - x) * CORES + i
+        cols = pl.ds(pl.multiple_of(j * md, md), md)
+        cross = dot3(nh[...], nl[...], dh[cols, :], dl[cols, :], NT)
+        norms = cn[cols, :].T[0:1, :]
+        for t in range(md // 128):
             lanes = slice(t * 128, (t + 1) * 128)
-            score[i, :, lanes] = (
+            score[j, :, lanes] = (
                 2.0 * cross[:, lanes] - rn[...] - norms[:, lanes]) * (1.0 / (D * EPS))
         return carry
 
-    lax.fori_loop(0, QUAD, score_body, 0)
+    lax.fori_loop(0, CORES, score_body, 0)
 
     lane = lax.broadcasted_iota(jnp.int32, (1, 128), 1)
-    sub = lax.broadcasted_iota(jnp.int32, (8, 1), 0)
+    RB, CB, SB = R // 128, C // 128, md // 128
     block = 128
 
     def row_pass(pot, weights):
+        def shift(j):
+            return jnp.concatenate([pot[j * SB + t:j * SB + t + 1] for t in range(SB)], axis=1)
+
         def body(i, carry):
             rows = pl.ds(pl.multiple_of(i * block, block), block)
-            vals = [score[j, rows, :] + (0.0 if pot is None else pot[:, j * md:(j + 1) * md])
+            vals = [score[j, rows, :] + (0.0 if pot is None else shift(j))
                     for j in range(QUAD)]
             peak = functools.reduce(jnp.maximum, vals)
             peak = jnp.max(peak, axis=1, keepdims=True)
@@ -255,16 +272,19 @@
         return rc(rs.at[ex, at], rs.at[ex, at], rss.at[ex, r], rsr.at[ex, at], group_dev(g2))
 
     def row_exchange(ex):
-        rs[ex, g] = st[...].T[0:8, :]
+        for k in range(RB):
+            turned = st[k * 128:(k + 1) * 128, :].T
+            rs[ex, g, k:k + 1, :] = turned[0:1]
+            rs[ex, g, RB + k:RB + k + 1, :] = turned[1:2]
         for r in range(1, G):
             row_copy(ex, r).start()
 
     def row_combine(ex):
         for r in range(1, G):
             row_copy(ex, r, True).wait_recv()
-        peaks = [rs[ex, k][0:1, :] for k in range(G)]
+        peaks = [rs[ex, k, 0:RB, :] for k in range(G)]
         top = functools.reduce(jnp.maximum, peaks)
-        total = sum(rs[ex, k][1:2, :] * jnp.exp(peaks[k] - top) for k in range(G))
+        total = sum(rs[ex, k, RB:2 * RB, :] * jnp.exp(peaks[k] - top) for k in range(G))
         return top, total
 
     def col_copy(ex, r, landed=False):
@@ -272,38 +292,35 @@
         at = q2 if landed else q
         return rc(cs.at[ex, at], cs.at[ex, at], css.at[ex, r], csr.at[ex, at], quad_dev(q2))
 
-    def spread(row):
-        return jnp.broadcast_to(row, (128, row.shape[1])).T
+    def spread(packed):
+        for k in range(RB):
+            st[k * 128:(k + 1) * 128, :] = jnp.broadcast_to(packed[k:k + 1], (128, 128)).T
 
     pot = None
     for step in range(ITERS):
         row_pass(pot, False)
         row_exchange(step)
         top, total = row_combine(step)
-        st[...] = spread(math.log(total_data) - (top + jnp.log(total)))
+        spread(math.log(total_data) - (top + jnp.log(total)))
         for j in range(QUAD):
-            for t in range(md // 128):
-                lanes = slice(t * 128, (t + 1) * 128)
+            for t in range(SB):
+                lanes, at = slice(t * 128, (t + 1) * 128), j * SB + t
                 val = score[j, :, lanes] + st[...]
                 peak = jnp.max(val, axis=0, keepdims=True)
                 total = jnp.sum(jnp.exp(val - peak), axis=0, keepdims=True)
-                cs[step, q, :, j * md + t * 128:j * md + (t + 1) * 128] = jnp.where(
-                    sub == 0, peak, total)
+                cs[step, q, at:at + 1, :] = peak
+                cs[step, q, CB + at:CB + at + 1, :] = total
         for r in range(1, QUAD):
             col_copy(step, r).start()
         for r in range(1, QUAD):
             col_copy(step, r, True).wait_recv()
-        peaks = [cs[step, k][0:1, :] for k in range(QUAD)]
+        peaks = [cs[step, k, 0:CB, :] for k in range(QUAD)]
         top = functools.reduce(jnp.maximum, peaks)
-        total = sum(cs[step, k][1:2, :] * jnp.exp(peaks[k] - top) for k in range(QUAD))
+        total = sum(cs[step, k, CB:2 * CB, :] * jnp.exp(peaks[k] - top) for k in range(QUAD))
         pot = math.log(total_noise) - (top + jnp.log(total))
 
     row_pass(pot, True)
     row_exchange(ITERS)
-    mine = st[...].T[0:1, :]
-    top, total = row_combine(ITERS)
-    st[...] = spread(jnp.exp(mine - top) / total)
-
     far, near = jnp.maximum(z, Z - 1 - z), jnp.minimum(z, Z - 1 - z)
     toward = jnp.where(Z - 1 - z >= z, 1, -1)
 
@@ -313,69 +330,83 @@
         flip = jnp.where(lax.rem(jnp.maximum(m, 0), 2) == 0, 1, -1)
         return z + toward * jnp.where(m < 0, far - n, late * flip)
 
-    def part_copy(zz, r):
+    half = nb // HALVES
+
+    def part_copy(zz, h, r, landed=False):
         y2 = lax.rem(y + r, Y)
-        return rc(part.at[zz, y2], yb.at[zz, y], ps.at[zz, r], pr.at[zz, y], dev(z, y2, x, c))
-
-    def part_landed(zz, r):
-        y2 = lax.rem(y + r, Y)
-        return rc(part.at[zz, y2], yb.at[zz, y2], ps.at[zz, r], pr.at[zz, y2], dev(z, y2, x, c))
-
-    def up_part(zz):
-        return rc(part.at[zz, y], ub.at[zz], us.at[zz], ur.at[zz], dev(z + 1, y, x, c))
-
-    def dn_part(zz):
-        return rc(part.at[zz, y], db.at[zz], vs.at[zz], vr.at[zz], dev(z - 1, y, x, c))
-
-    def multiply(zz):
+        rows, at = pl.ds(pl.multiple_of(h * half, half), half), y2 if landed else y
+        return rc(part.at[zz, y2, rows], yb.at[zz, at, rows],
+                  ps.at[zz, h, r], pr.at[zz, h, at], dev(z, y2, x, c))
+
+    def up_part(zz, h):
+        rows = pl.ds(pl.multiple_of(h * half, half), half)
+        return rc(part.at[zz, y, rows], ub.at[zz, rows], us.at[zz, h], ur.at[zz, h],
+                  dev(z + 1, y, x, c))
+
+    def dn_part(zz, h):
+        rows = pl.ds(pl.multiple_of(h * half, half), half)
+        return rc(part.at[zz, y, rows], db.at[zz, rows], vs.at[zz, h], vr.at[zz, h],
+                  dev(z - 1, y, x, c))
+
+    def multiply(zz, scaled):
         rows = pl.ds(pl.multiple_of(zz * (Y * nb), Y * nb), Y * nb)
         both = jnp.concatenate([wh[rows, :], wl[rows, :]], axis=0)
-        scale = st[rows, :]
         for n in range(D // 256):
             lanes = slice(n * 256, (n + 1) * 256)
             numer = dot3_stacked(both, dh[:, lanes], dl[:, lanes], NN)
             for t in range(2):
-                piece = numer[:, t * 128:(t + 1) * 128] * scale
+                piece = numer[:, t * 128:(t + 1) * 128]
+                if scaled:
+                    piece = piece * st[rows, :]
                 for k in range(Y):
                     part[zz, k, :, n * 256 + t * 128:n * 256 + (t + 1) * 128] = (
                         piece[k * nb:(k + 1) * nb])
 
-    def reduce_step(zz):
-        for r in range(1, Y):
-            part[zz, y] += yb[zz, lax.rem(y + r, Y)]
+    def part_sends(p):
+        for r in range(1, Y):
+            part_copy(order(lax.div(p, HALVES)), lax.rem(p, HALVES), r).start()
+
+    first = order(jnp.int32(0))
+    multiply(first, False)
+    top, total = row_combine(ITERS)
+    spread(jnp.exp(rs[ITERS, g, 0:RB, :] - top) / total)
+    for k in range(Y):
+        scale = st[pl.ds(pl.multiple_of(first * (Y * nb), Y * nb) + k * nb, nb), :]
+        for t in range(D // 128):
+            part[first, k, :, t * 128:(t + 1) * 128] *= scale
+    for p in range(HALVES):
+        part_sends(jnp.int32(p))
+
+    def multiply_body(n, carry):
+        multiply(order(n), True)
+        return carry
+
+    lax.fori_loop(1, Z, multiply_body, 0)
+
+    def reduce_body(p, carry):
+        zz, h = order(lax.div(p, HALVES)), lax.rem(p, HALVES)
+        rows = pl.ds(pl.multiple_of(h * half, half), half)
+        for r in range(1, Y):
+            part_copy(zz, h, r, True).wait_recv()
+        pl.when(p + HALVES < Z * HALVES)(lambda: part_sends(p + HALVES))
+        for r in range(1, Y):
+            part[zz, y, rows, :] += yb[zz, lax.rem(y + r, Y), rows, :]
 
         @pl.when((zz >= z) & (z > 0))
         def _():
-            up_part(zz).wait_recv()
-            part[zz, y] += ub[zz]
+            up_part(zz, h).wait_recv()
+            part[zz, y, rows, :] += ub[zz, rows, :]
 
         @pl.when((zz <= z) & (z + 1 < Z))
         def _():
-            dn_part(zz).wait_recv()
-            part[zz, y] += db[zz]
-
-        pl.when(zz > z)(lambda: up_part(zz).start())
-        pl.when(zz < z)(lambda: dn_part(zz).start())
-
-    def reduce_body(n, carry):
-        zz, last = order(n), order(n - 1)
-        pl.when(n < Z)(lambda: multiply(zz))
-
-        @pl.when(n > 0)
-        def _():
-            for r in range(1, Y):
-                part_copy(last, r).wait_send()
-                part_landed(last, r).wait_recv()
-
-        @pl.when(n < Z)
-        def _():
-            for r in range(1, Y):
-                part_copy(zz, r).start()
-
-        pl.when(n > 0)(lambda: reduce_step(last))
+            dn_part(zz, h).wait_recv()
+            part[zz, y, rows, :] += db[zz, rows, :]
+
+        pl.when(zz > z)(lambda: up_part(zz, h).start())
+        pl.when(zz < z)(lambda: dn_part(zz, h).start())
         return carry
 
-    lax.fori_loop(0, Z + 1, reduce_body, 0)
+    lax.fori_loop(0, Z * HALVES, reduce_body, 0)
     out_ref[...] = part[z, y]
 
     for k in range(PIECES):
@@ -394,8 +425,11 @@
     for zz in range(Z):
         for r in range(1, Y):
             y_copy(zz, r).wait_send()
-        pl.when(zz > z)(lambda: up_part(zz).wait_send())
-        pl.when(zz < z)(lambda: dn_part(zz).wait_send())
+        for h in range(HALVES):
+            for r in range(1, Y):
+                part_copy(zz, h, r).wait_send()
+            pl.when(zz > z)(lambda: up_part(zz, h).wait_send())
+            pl.when(zz < z)(lambda: dn_part(zz, h).wait_send())
 
 
 def targets_of(Z, Y, noise, data):
@@ -416,13 +450,14 @@
             V((R, 128), f32), V((C, 128), f32),
             V((QUAD, R, md), f32), V((R, 128), f32),
             V((R, C), bf16), V((R, C), bf16),
-            V((ITERS + 1, G, 8, R), f32), V((ITERS, QUAD, 8, C), f32),
+            V((ITERS + 1, G, R // 64, 128), f32), V((ITERS, QUAD, C // 64, 128), f32),
             V((Z, Y, nb, D), f32), V((Z, Y, nb, D), f32), V((Z, nb, D), f32), V((Z, nb, D), f32),
             dma((Z,)), dma((Z,)), dma((Z,)), dma((Z,)),
             dma((Z, Y)), dma((Z, Y)),
             dma((PIECES,)), dma((PIECES,)), dma((2,)), dma((PIECES,)), dma((PIECES,)),
             dma((ITERS + 1, G)), dma((ITERS + 1, G)), dma((ITERS, QUAD)), dma((ITERS, QUAD)),
-            dma((Z, Y)), dma((Z, Y)), dma((Z,)), dma((Z,)), dma((Z,)), dma((Z,)),
+            dma((Z, HALVES, Y)), dma((Z, HALVES, Y)),
+            dma((Z, HALVES)), dma((Z, HALVES)), dma((Z, HALVES)), dma((Z, HALVES)),
         ],
         compiler_params=pltpu.CompilerParams(
             collective_id=0, has_side_effects=True, vmem_limit_bytes=60 * 1024 * 1024),

time: 146 us -> 137 us (0.938)
  Pallas kernels: 143 us -> 133 us
    pallas_call x1, Pallas kernels: 143 us -> 133 us  [targets_of(): pl.pallas_call(functools.partial(kernel, Z, Y), out_shape=jax.ShapeDtypeS...]
where the time goes in v3:
time: 137 us; the launch traced here: 136 us
  Pallas kernels  133 us (97%)
  other arithmetic  2.73 us (2%)
    pallas_call x1, Pallas kernels, targets_of(): pl.pallas_call(functools.partial(kernel, Z, Y), out_shape=jax.ShapeDtypeS...  133 us

profile of v3, /device:TPU:0, one launch (start us, length us, event | category | flops | bytes accessed | tf_op | source)
XLA Modules:
  0.0 136.4 jit_solution(10003008876412683384)
XLA Ops:
  0.6 0.7 broadcast_subtract_fusion
  1.3 0.0 copy-start
  1.3 0.0 copy-start.1
  1.3 133.0 %shard_map.50 = f32[64,2048]{1,0:T(8,128)} custom-call(f32[64,2048]{1,0:T(8,128)} %noise_ref.1, f32[256,2048]{1,0:T(8,128)} %data_ref.1), custom_call_target="tpu_custom_call" | custom-call | flops 12884901888 | bytes 25165824 | tf_op jit(solution)/shard_map/pallas_call | solution.py:442
  134.3 0.0 copy-done
  134.3 0.0 copy-done.1
  134.3 2.1 %fusion = (f32[64,2048]{1,0:T(8,128)}, f32[64,2048]{1,0:T(8,128)}) fusion(f32[64,2048]{1,0:T(8,128)} %shard_map.50, f32[64,2048]{1,0:T(8,128)S(1)} %copy-done, f32[64]{0:T(128)S(1)} %copy-done.1, f32[64]{0:T(128)S(1)} %broadcast_subtract_fusion), kind=kLoop, calls=%fused_computation.2 | loop fusion | flops 524288 | bytes 2097664 | tf_op jit(solution)/shard_map/sub | solution.py:472
Async XLA Ops:
  1.3 133.0 %copy-start = (f32[64,2048]{1,0:T(8,128)S(1)}, f32[64,2048]{1,0:T(8,128)}, u32[]{:S(2)}) copy-start(f32[64,2048]{1,0:T(8,128)} %noise_ref.1) | copy-start | bytes 1572868
  1.3 133.0 %copy-start.1 = (f32[64]{0:T(128)S(1)}, f32[64]{0:T(128)}, u32[]{:S(2)}) copy-start(f32[64]{0:T(128)} %param.5) | copy-start | bytes 772

commit v4 on v3

--- a/solution.py
+++ b/solution.py
@@ -14,6 +14,7 @@
 CORES = 2
 QUAD = PAIR * CORES
 PIECES = 4
+TAIL = 8
 HALVES = 2
 f32 = jnp.float32
 bf16 = jnp.bfloat16
@@ -40,7 +41,7 @@
 
 def kernel(
     Z, Y, noise_ref, data_ref, out_ref,
-    nf, df, nh, nl, dh, dl, rn, cn, score, st, wh, wl, rs, cs, part, yb, ub, db,
+    nf, df, nh, nl, dh, dl, rn, cn, score, st, wh, wl, rs, cs, part, yb, ub, db, ut, dt,
     up_s, up_r, dn_s, dn_r, ys, yr, xs, xr, sib, fs, fr, rss, rsr, css, csr,
     ps, pr, us, ur, vs, vr,
 ):
@@ -330,22 +331,31 @@
         flip = jnp.where(lax.rem(jnp.maximum(m, 0), 2) == 0, 1, -1)
         return z + toward * jnp.where(m < 0, far - n, late * flip)
 
-    half = nb // HALVES
+    main = nb - TAIL
+    cutat = -(-main // (8 * HALVES)) * 8
+    pieces = [pl.ds(0, cutat), pl.ds(cutat, main - cutat)]
+    tail = pl.ds(main, TAIL)
 
     def part_copy(zz, h, r, landed=False):
         y2 = lax.rem(y + r, Y)
-        rows, at = pl.ds(pl.multiple_of(h * half, half), half), y2 if landed else y
+        rows, at = (pieces + [tail])[h], y2 if landed else y
         return rc(part.at[zz, y2, rows], yb.at[zz, at, rows],
                   ps.at[zz, h, r], pr.at[zz, h, at], dev(z, y2, x, c))
 
     def up_part(zz, h):
-        rows = pl.ds(pl.multiple_of(h * half, half), half)
-        return rc(part.at[zz, y, rows], ub.at[zz, rows], us.at[zz, h], ur.at[zz, h],
+        return rc(part.at[zz, y, pieces[h]], ub.at[zz, pieces[h]], us.at[zz, h], ur.at[zz, h],
                   dev(z + 1, y, x, c))
 
     def dn_part(zz, h):
-        rows = pl.ds(pl.multiple_of(h * half, half), half)
-        return rc(part.at[zz, y, rows], db.at[zz, rows], vs.at[zz, h], vr.at[zz, h],
+        return rc(part.at[zz, y, pieces[h]], db.at[zz, pieces[h]], vs.at[zz, h], vr.at[zz, h],
+                  dev(z - 1, y, x, c))
+
+    def up_tail(zz):
+        return rc(part.at[zz, :, tail], ut.at[zz], us.at[zz, HALVES], ur.at[zz, HALVES],
+                  dev(z + 1, y, x, c))
+
+    def dn_tail(zz):
+        return rc(part.at[zz, :, tail], dt.at[zz], vs.at[zz, HALVES], vr.at[zz, HALVES],
                   dev(z - 1, y, x, c))
 
     def multiply(zz, scaled):
@@ -362,9 +372,12 @@
                     part[zz, k, :, n * 256 + t * 128:n * 256 + (t + 1) * 128] = (
                         piece[k * nb:(k + 1) * nb])
 
-    def part_sends(p):
-        for r in range(1, Y):
-            part_copy(order(lax.div(p, HALVES)), lax.rem(p, HALVES), r).start()
+    def launch(zz):
+        for h in range(HALVES):
+            for r in range(1, Y):
+                part_copy(zz, h, r).start()
+        pl.when((zz > z) & (z == 0))(lambda: up_tail(zz).start())
+        pl.when((zz < z) & (z == Z - 1))(lambda: dn_tail(zz).start())
 
     first = order(jnp.int32(0))
     multiply(first, False)
@@ -374,41 +387,69 @@
         scale = st[pl.ds(pl.multiple_of(first * (Y * nb), Y * nb) + k * nb, nb), :]
         for t in range(D // 128):
             part[first, k, :, t * 128:(t + 1) * 128] *= scale
-    for p in range(HALVES):
-        part_sends(jnp.int32(p))
+    launch(first)
 
     def multiply_body(n, carry):
         multiply(order(n), True)
+        launch(order(n))
         return carry
 
     lax.fori_loop(1, Z, multiply_body, 0)
 
-    def reduce_body(p, carry):
-        zz, h = order(lax.div(p, HALVES)), lax.rem(p, HALVES)
-        rows = pl.ds(pl.multiple_of(h * half, half), half)
-        for r in range(1, Y):
-            part_copy(zz, h, r, True).wait_recv()
-        pl.when(p + HALVES < Z * HALVES)(lambda: part_sends(p + HALVES))
-        for r in range(1, Y):
-            part[zz, y, rows, :] += yb[zz, lax.rem(y + r, Y), rows, :]
+    def tail_body(n, carry):
+        zz = order(n)
 
         @pl.when((zz >= z) & (z > 0))
         def _():
-            up_part(zz, h).wait_recv()
-            part[zz, y, rows, :] += ub[zz, rows, :]
+            up_tail(zz).wait_recv()
+            part[zz, :, tail, :] += ut[zz]
 
         @pl.when((zz <= z) & (z + 1 < Z))
         def _():
-            dn_part(zz, h).wait_recv()
-            part[zz, y, rows, :] += db[zz, rows, :]
-
-        pl.when(zz > z)(lambda: up_part(zz, h).start())
-        pl.when(zz < z)(lambda: dn_part(zz, h).start())
+            dn_tail(zz).wait_recv()
+            part[zz, :, tail, :] += dt[zz]
+
+        pl.when((zz > z) & (z > 0))(lambda: up_tail(zz).start())
+        pl.when((zz < z) & (z + 1 < Z))(lambda: dn_tail(zz).start())
+
+        @pl.when(zz == z)
+        def _():
+            for r in range(1, Y):
+                part_copy(zz, HALVES, r).start()
+
         return carry
 
-    lax.fori_loop(0, Z * HALVES, reduce_body, 0)
+    lax.fori_loop(0, Z, tail_body, 0)
+
+    def reduce_body(n, carry):
+        zz = order(n)
+        for h, rows in enumerate(pieces):
+            for r in range(1, Y):
+                part_copy(zz, h, r, True).wait_recv()
+                part[zz, y, rows, :] += yb[zz, lax.rem(y + r, Y), rows, :]
+
+            @pl.when((zz >= z) & (z > 0))
+            def _():
+                up_part(zz, h).wait_recv()
+                part[zz, y, rows, :] += ub[zz, rows, :]
+
+            @pl.when((zz <= z) & (z + 1 < Z))
+            def _():
+                dn_part(zz, h).wait_recv()
+                part[zz, y, rows, :] += db[zz, rows, :]
+
+            pl.when(zz > z)(lambda: up_part(zz, h).start())
+            pl.when(zz < z)(lambda: dn_part(zz, h).start())
+        return carry
+
+    lax.fori_loop(0, Z, reduce_body, 0)
+    for r in range(1, Y):
+        part_copy(z, HALVES, r, True).wait_recv()
+        part[z, y, tail, :] += yb[z, lax.rem(y + r, Y), tail, :]
     out_ref[...] = part[z, y]
 
+    for r in range(1, Y):
+        part_copy(z, HALVES, r).wait_send()
     for k in range(PIECES):
         data_send(k).wait_send()
         data_forward(k).wait_send()
@@ -430,6 +471,8 @@
                 part_copy(zz, h, r).wait_send()
             pl.when(zz > z)(lambda: up_part(zz, h).wait_send())
             pl.when(zz < z)(lambda: dn_part(zz, h).wait_send())
+        pl.when(zz > z)(lambda: up_tail(zz).wait_send())
+        pl.when(zz < z)(lambda: dn_tail(zz).wait_send())
 
 
 def targets_of(Z, Y, noise, data):
@@ -452,12 +495,14 @@
             V((R, C), bf16), V((R, C), bf16),
             V((ITERS + 1, G, R // 64, 128), f32), V((ITERS, QUAD, C // 64, 128), f32),
             V((Z, Y, nb, D), f32), V((Z, Y, nb, D), f32), V((Z, nb, D), f32), V((Z, nb, D), f32),
+            V((Z, Y, TAIL, D), f32), V((Z, Y, TAIL, D), f32),
             dma((Z,)), dma((Z,)), dma((Z,)), dma((Z,)),
             dma((Z, Y)), dma((Z, Y)),
             dma((PIECES,)), dma((PIECES,)), dma((2,)), dma((PIECES,)), dma((PIECES,)),
             dma((ITERS + 1, G)), dma((ITERS + 1, G)), dma((ITERS, QUAD)), dma((ITERS, QUAD)),
-            dma((Z, HALVES, Y)), dma((Z, HALVES, Y)),
-            dma((Z, HALVES)), dma((Z, HALVES)), dma((Z, HALVES)), dma((Z, HALVES)),
+            dma((Z, HALVES + 1, Y)), dma((Z, HALVES + 1, Y)),
+            dma((Z, HALVES + 1)), dma((Z, HALVES + 1)),
+            dma((Z, HALVES + 1)), dma((Z, HALVES + 1)),
         ],
         compiler_params=pltpu.CompilerParams(
             collective_id=0, has_side_effects=True, vmem_limit_bytes=60 * 1024 * 1024),

time: 137 us -> 136 us (level)
  no operation moved by 1% of the time
where the time goes in v4:
time: 136 us; the launch traced here: 135 us
  Pallas kernels  132 us (97%)
  other arithmetic  2.73 us (2%)
    pallas_call x1, Pallas kernels, targets_of(): pl.pallas_call(functools.partial(kernel, Z, Y), out_shape=jax.ShapeDtypeS...  132 us

profile of v4, /device:TPU:0, one launch (start us, length us, event | category | flops | bytes accessed | tf_op | source)
XLA Modules:
  0.0 135.5 jit_solution(12129219543545745459)
XLA Ops:
  0.6 0.7 broadcast_subtract_fusion
  1.3 0.0 copy-start
  1.3 0.0 copy-start.1
  1.3 132.1 %shard_map.50 = f32[64,2048]{1,0:T(8,128)} custom-call(f32[64,2048]{1,0:T(8,128)} %noise_ref.1, f32[256,2048]{1,0:T(8,128)} %data_ref.1), custom_call_target="tpu_custom_call" | custom-call | flops 12884901888 | bytes 25165824 | tf_op jit(solution)/shard_map/pallas_call | solution.py:485
  133.4 0.0 copy-done
  133.4 0.0 copy-done.1
  133.4 2.1 %fusion = (f32[64,2048]{1,0:T(8,128)}, f32[64,2048]{1,0:T(8,128)}) fusion(f32[64,2048]{1,0:T(8,128)} %shard_map.50, f32[64,2048]{1,0:T(8,128)S(1)} %copy-done, f32[64]{0:T(128)S(1)} %copy-done.1, f32[64]{0:T(128)S(1)} %broadcast_subtract_fusion), kind=kLoop, calls=%fused_computation.2 | loop fusion | flops 524288 | bytes 2097664 | tf_op jit(solution)/shard_map/sub | solution.py:517
Async XLA Ops:
  1.3 132.1 %copy-start = (f32[64,2048]{1,0:T(8,128)S(1)}, f32[64,2048]{1,0:T(8,128)}, u32[]{:S(2)}) copy-start(f32[64,2048]{1,0:T(8,128)} %noise_ref.1) | copy-start | bytes 1572868
  1.3 132.1 %copy-start.1 = (f32[64]{0:T(128)S(1)}, f32[64]{0:T(128)}, u32[]{:S(2)}) copy-start(f32[64]{0:T(128)} %param.5) | copy-start | bytes 772

commit v5 on v4

--- a/solution.py
+++ b/solution.py
@@ -13,6 +13,7 @@
 PAIR = 2
 CORES = 2
 QUAD = PAIR * CORES
+WIDE = 128 * CORES
 PIECES = 4
 TAIL = 8
 HALVES = 2
@@ -40,16 +41,18 @@
 
 
 def kernel(
-    Z, Y, noise_ref, data_ref, out_ref,
+    Z, Y, noise_ref, data_ref, times_ref, path_ref, velocity_ref,
     nf, df, nh, nl, dh, dl, rn, cn, score, st, wh, wl, rs, cs, part, yb, ub, db, ut, dt,
     up_s, up_r, dn_s, dn_r, ys, yr, xs, xr, sib, fs, fr, rss, rsr, css, csr,
-    ps, pr, us, ur, vs, vr,
+    ps, pr, us, ur, vs, vr, own,
 ):
     nb, D = noise_ref.shape
     md = data_ref.shape[0]
     G = Z * Y
     R, C = G * nb, QUAD * md
     mc = md // PIECES
+    NB = C // WIDE
+    NX = NB // PAIR
     total_noise, total_data = R * QUAD, C * G
     z = lax.axis_index("row")
     col = lax.axis_index("col")
@@ -74,6 +77,20 @@
     def quad_dev(q2):
         return dev(z, y, lax.div(q2, CORES), lax.rem(q2, CORES))
 
+    far, near = jnp.maximum(z, Z - 1 - z), jnp.minimum(z, Z - 1 - z)
+    toward = jnp.where(Z - 1 - z >= z, 1, -1)
+
+    def order(n):
+        m = n - (far - near)
+        late = near - lax.div(jnp.maximum(m, 0), 2)
+        flip = jnp.where(lax.rem(jnp.maximum(m, 0), 2) == 0, 1, -1)
+        return z + toward * jnp.where(m < 0, far - n, late * flip)
+
+    own_noise = pltpu.make_async_copy(noise_ref, nf.at[g], own.at[0])
+    own_data = pltpu.make_async_copy(data_ref, df.at[q], own.at[1])
+    own_noise.start()
+    own_data.start()
+
     barrier = pltpu.get_barrier_semaphore()
     for r in range(1, G):
         pl.semaphore_signal(barrier, inc=1, device_id=group_dev(lax.rem(g + r, G)),
@@ -130,12 +147,10 @@
         data_send(k).start()
     sib_copy = rc(data_ref, df.at[q], sib.at[0], sib.at[1], c_dev)
     sib_copy.start()
-    nf[g] = noise_ref[...]
+    own_noise.wait()
     y_sends(z)
     pl.when(z + 1 < Z)(lambda: up_copy(z, 0).start())
     pl.when(z > 0)(lambda: dn_copy(z, 0).start())
-    df[q] = data_ref[...]
-
     def convert(src, slot, base, at, count, high, low, norm):
         step = min(32, count)
 
@@ -155,22 +170,31 @@
         convert(nf, slot, 0, slot * nb, nb, nh, nl, rn)
 
     def convert_data(slot, k, count):
-        convert(df, slot, k * mc, slot * md + k * mc, count, dh, dl, cn)
+        step = min(count, 128)
+        for base in range(k * mc, k * mc + count, step):
+            at = (lax.div(slot, CORES) * (NX * WIDE) + lax.rem(slot, CORES) * 128
+                  + base // 128 * WIDE + base % 128)
+            convert(df, slot, base, at, step, dh, dl, cn)
 
     convert_noise(g)
+    own_data.wait()
     convert_data(q, 0, md)
     rc(data_ref, df.at[qc], sib.at[0], sib.at[1], c_dev).wait_recv()
     convert_data(qc, 0, md)
 
-    def score_block(at, count, j):
-        rows, cols = pl.ds(at, count), pl.ds(pl.multiple_of(j * md, md), md)
-        both = jnp.concatenate([nh[rows, :], nl[rows, :]], axis=0)
-        cross = dot3_stacked(both, dh[cols, :], dl[cols, :], NT)
+    def score_finish(cross, at, count, j):
+        rows, cols = pl.ds(at, count), pl.ds(pl.multiple_of(j * WIDE, WIDE), WIDE)
         norms = cn[cols, :].T[0:1, :]
-        for t in range(md // 128):
+        for t in range(WIDE // 128):
             lanes = slice(t * 128, (t + 1) * 128)
             score[j, rows, lanes] = (
                 2.0 * cross[:, lanes] - rn[rows, :] - norms[:, lanes]) * (1.0 / (D * EPS))
+
+    def score_pair(zz, j):
+        at, count = pl.multiple_of(zz * (Y * nb), Y * nb), Y * nb
+        rows, cols = pl.ds(at, count), pl.ds(pl.multiple_of(j * WIDE, WIDE), WIDE)
+        both = jnp.concatenate([nh[rows, :], nl[rows, :]], axis=0)
+        score_finish(dot3_stacked(both, dh[cols, :], dl[cols, :], NT), at, count, j)
 
     def y_arrivals(zz):
         for r in range(1, Y):
@@ -178,15 +202,14 @@
             convert_noise(zz * Y + lax.rem(y + r, Y))
 
         def body(i, carry):
-            score_block(pl.multiple_of(zz * (Y * nb), Y * nb), Y * nb, x * CORES + i)
+            score_pair(zz, x * NX + i)
             return carry
 
-        lax.fori_loop(0, CORES, body, 0)
+        lax.fori_loop(0, NX, body, 0)
 
     def data_piece(k):
         data_recv(k).wait_recv()
         data_forward(k).start()
-        convert_data(qx, k, mc)
 
     def data_piece_forwarded(k):
         data_forwarded(k).wait_recv()
@@ -214,35 +237,39 @@
         pl.when(lo >= 0)(lambda: convert_noise(lo * Y + y))
         pl.when(hi < Z)(lambda: convert_noise(hi * Y + y))
         if s == Z - 1:
-            for k in range(PIECES - 1):
+            for k in range(PIECES // 2):
                 data_piece(k)
-            for k in range(PIECES - 1):
+                convert_data(qx, k, mc)
+            for k in range(PIECES // 2):
                 data_piece_forwarded(k)
         if s == 1:
-            y_arrivals(z)
+            pl.when(z != order(0))(lambda: y_arrivals(z))
         else:
-            pl.when(lo + 1 >= 0)(lambda: y_arrivals(lo + 1))
-            pl.when(hi - 1 < Z)(lambda: y_arrivals(hi - 1))
-    pl.when(z - Z + 1 >= 0)(lambda: y_arrivals(z - Z + 1))
-    pl.when(z + Z - 1 < Z)(lambda: y_arrivals(z + Z - 1))
-    data_piece(PIECES - 1)
-    data_piece_forwarded(PIECES - 1)
-
-    def score_body(i, carry):
-        j = (1 - x) * CORES + i
-        cols = pl.ds(pl.multiple_of(j * md, md), md)
-        cross = dot3(nh[...], nl[...], dh[cols, :], dl[cols, :], NT)
-        norms = cn[cols, :].T[0:1, :]
-        for t in range(md // 128):
-            lanes = slice(t * 128, (t + 1) * 128)
-            score[j, :, lanes] = (
-                2.0 * cross[:, lanes] - rn[...] - norms[:, lanes]) * (1.0 / (D * EPS))
+            pl.when((lo + 1 >= 0) & (lo + 1 != order(0)))(lambda: y_arrivals(lo + 1))
+            pl.when((hi - 1 < Z) & (hi - 1 != order(0)))(lambda: y_arrivals(hi - 1))
+
+    def early_body(n, carry):
+        for i in range(NX - 1):
+            score_pair(order(n), (1 - x) * NX + i)
         return carry
 
-    lax.fori_loop(0, CORES, score_body, 0)
+    lax.fori_loop(1, Z, early_body, 0)
+    for k in range(PIECES // 2, PIECES):
+        data_piece(k)
+        if k < PIECES - 1:
+            convert_data(qx, k, mc)
+    y_arrivals(order(0))
+    early_body(0, 0)
+    convert_data(qx, PIECES - 1, mc)
+    for k in range(PIECES // 2, PIECES):
+        data_piece_forwarded(k)
+
+    last = (1 - x) * NX + NX - 1
+    cols = pl.ds(pl.multiple_of(last * WIDE, WIDE), WIDE)
+    score_finish(dot3(nh[...], nl[...], dh[cols, :], dl[cols, :], NT), 0, R, last)
 
     lane = lax.broadcasted_iota(jnp.int32, (1, 128), 1)
-    RB, CB, SB = R // 128, C // 128, md // 128
+    RB, CB, SB = R // 128, C // 128, WIDE // 128
     block = 128
 
     def row_pass(pot, weights):
@@ -252,17 +279,17 @@
         def body(i, carry):
             rows = pl.ds(pl.multiple_of(i * block, block), block)
             vals = [score[j, rows, :] + (0.0 if pot is None else shift(j))
-                    for j in range(QUAD)]
+                    for j in range(NB)]
             peak = functools.reduce(jnp.maximum, vals)
             peak = jnp.max(peak, axis=1, keepdims=True)
             exps = [jnp.exp(v - peak) for v in vals]
             total = jnp.sum(functools.reduce(jnp.add, exps), axis=1, keepdims=True)
             st[rows, :] = jnp.where(lane == 0, peak, total)
             if weights:
-                for j in range(QUAD):
+                for j in range(NB):
                     h, l = split(exps[j])
-                    wh[rows, j * md:(j + 1) * md] = h
-                    wl[rows, j * md:(j + 1) * md] = l
+                    wh[rows, j * WIDE:(j + 1) * WIDE] = h
+                    wl[rows, j * WIDE:(j + 1) * WIDE] = l
             return carry
 
         lax.fori_loop(0, R // block, body, 0)
@@ -303,7 +330,7 @@
         row_exchange(step)
         top, total = row_combine(step)
         spread(math.log(total_data) - (top + jnp.log(total)))
-        for j in range(QUAD):
+        for j in range(NB):
             for t in range(SB):
                 lanes, at = slice(t * 128, (t + 1) * 128), j * SB + t
                 val = score[j, :, lanes] + st[...]
@@ -322,15 +349,6 @@
 
     row_pass(pot, True)
     row_exchange(ITERS)
-    far, near = jnp.maximum(z, Z - 1 - z), jnp.minimum(z, Z - 1 - z)
-    toward = jnp.where(Z - 1 - z >= z, 1, -1)
-
-    def order(n):
-        m = n - (far - near)
-        late = near - lax.div(jnp.maximum(m, 0), 2)
-        flip = jnp.where(lax.rem(jnp.maximum(m, 0), 2) == 0, 1, -1)
-        return z + toward * jnp.where(m < 0, far - n, late * flip)
-
     main = nb - TAIL
     cutat = -(-main // (8 * HALVES)) * 8
     pieces = [pl.ds(0, cutat), pl.ds(cutat, main - cutat)]
@@ -446,7 +464,14 @@
     for r in range(1, Y):
         part_copy(z, HALVES, r, True).wait_recv()
         part[z, y, tail, :] += yb[z, lax.rem(y + r, Y), tail, :]
-    out_ref[...] = part[z, y]
+
+    wide_times = jnp.concatenate([times_ref[...], jnp.zeros((1, 128 - nb), f32)], axis=1)
+    share = jnp.broadcast_to(wide_times, (128, 128)).T[0:nb]
+    for t in range(D // 128):
+        lanes = slice(t * 128, (t + 1) * 128)
+        noise, targets = nf[g, :, lanes], part[z, y, :, lanes]
+        path_ref[:, lanes] = (1.0 - share) * noise + share * targets
+        velocity_ref[:, lanes] = targets - noise
 
     for r in range(1, Y):
         part_copy(z, HALVES, r).wait_send()
@@ -475,7 +500,7 @@
         pl.when(zz < z)(lambda: dn_tail(zz).wait_send())
 
 
-def targets_of(Z, Y, noise, data):
+def per_device(Z, Y, noise, data, times):
     nb, D = noise.shape
     md = data.shape[0]
     G = Z * Y
@@ -484,14 +509,14 @@
     flops = 2 * 6 * R * C * D
     return pl.pallas_call(
         functools.partial(kernel, Z, Y),
-        out_shape=jax.ShapeDtypeStruct((nb, D), f32),
-        in_specs=[pl.BlockSpec(memory_space=pltpu.VMEM)] * 2,
-        out_specs=pl.BlockSpec(memory_space=pltpu.VMEM),
+        out_shape=[jax.ShapeDtypeStruct((nb, D), f32)] * 2,
+        in_specs=[pl.BlockSpec(memory_space=pl.ANY)] * 2 + [pl.BlockSpec(memory_space=pltpu.VMEM)],
+        out_specs=[pl.BlockSpec(memory_space=pltpu.VMEM)] * 2,
         scratch_shapes=[
             V((G, nb, D), f32), V((QUAD, md, D), f32),
             V((R, D), bf16), V((R, D), bf16), V((C, D), bf16), V((C, D), bf16),
             V((R, 128), f32), V((C, 128), f32),
-            V((QUAD, R, md), f32), V((R, 128), f32),
+            V((C // WIDE, R, WIDE), f32), V((R, 128), f32),
             V((R, C), bf16), V((R, C), bf16),
             V((ITERS + 1, G, R // 64, 128), f32), V((ITERS, QUAD, C // 64, 128), f32),
             V((Z, Y, nb, D), f32), V((Z, Y, nb, D), f32), V((Z, nb, D), f32), V((Z, nb, D), f32),
@@ -502,19 +527,13 @@
             dma((ITERS + 1, G)), dma((ITERS + 1, G)), dma((ITERS, QUAD)), dma((ITERS, QUAD)),
             dma((Z, HALVES + 1, Y)), dma((Z, HALVES + 1, Y)),
             dma((Z, HALVES + 1)), dma((Z, HALVES + 1)),
-            dma((Z, HALVES + 1)), dma((Z, HALVES + 1)),
+            dma((Z, HALVES + 1)), dma((Z, HALVES + 1)), dma((2,)),
         ],
         compiler_params=pltpu.CompilerParams(
             collective_id=0, has_side_effects=True, vmem_limit_bytes=60 * 1024 * 1024),
         cost_estimate=pl.CostEstimate(
             flops=flops, bytes_accessed=8 * (R + C) * D, transcendentals=5 * R * C),
-    )(noise, data)
-
-
-def per_device(Z, Y, noise, data, times):
-    targets = targets_of(Z, Y, noise, data)
-    path = (1.0 - times)[:, None] * noise + times[:, None] * targets
-    return (path, targets - noise)
+    )(noise, data, times.reshape(1, nb))
 
 
 def solution(mesh):

time: 136 us -> 137 us (level)
  local copies, waits for them, and re-layouts: 0.01 us -> 3.74 us
  other arithmetic: 2.73 us -> 0 us
    unnamed x4 -> x2, local copies, waits for them, and re-layouts: 0.01 us -> 3.74 us
    sub x2 -> x0, other arithmetic: 2.73 us -> none  [the longest x1 2.07 us: per_device(): return (path, targets - noise)]
where the time goes in v5:
time: 137 us; the launch traced here: 136 us
  Pallas kernels  132 us (96%)
  local copies, waits for them, and re-layouts  3.74 us (3%)
    pallas_call x1, Pallas kernels, per_device(): pl.pallas_call(functools.partial(kernel, Z, Y), out_shape=[jax.ShapeDtype...  132 us
    unnamed x2, local copies, waits for them, and re-layouts  3.74 us

profile of v5, /device:TPU:0, one launch (start us, length us, event | category | flops | bytes accessed | tf_op | source)
XLA Modules:
  0.0 136.3 jit_solution(13822406042744824312)
XLA Ops:
  0.6 132.0 %shard_map.50 = (f32[64,2048]{1,0:T(8,128)}, f32[64,2048]{1,0:T(8,128)}) custom-call(f32[64,2048]{1,0:T(8,128)} %noise_ref.1, f32[256,2048]{1,0:T(8,128)} %data_ref.1, f32[1,64]{1,0:T(1,128)} %bitcast.1), custom_call_target="tpu_custom_call" | custom-call | flops 12884901888 | bytes 25165824 | tf_op jit(solution)/shard_map/pallas_call | solution.py:510
  132.6 1.9 %copy.7 = f32[64,2048]{1,0:T(8,128)} copy(f32[64,2048]{1,0:T(8,128)} %get-tuple-element.4) | data formatting | bytes 1048576
  134.5 1.9 %copy.8 = f32[64,2048]{1,0:T(8,128)} copy(f32[64,2048]{1,0:T(8,128)} %get-tuple-element.5) | data formatting | bytes 1048576

commit v6 on v5

--- a/solution.py
+++ b/solution.py
@@ -41,8 +41,8 @@
 
 
 def kernel(
-    Z, Y, noise_ref, data_ref, times_ref, path_ref, velocity_ref,
-    nf, df, nh, nl, dh, dl, rn, cn, score, st, wh, wl, rs, cs, part, yb, ub, db, ut, dt,
+    Z, Y, noise_ref, data_ref, out_ref,
+    nf, df, nh, nl, dh, dl, rn, cn, score, st, wh, wl, rs, cs, part, yb, ub, db, ut, dt, sc,
     up_s, up_r, dn_s, dn_r, ys, yr, xs, xr, sib, fs, fr, rss, rsr, css, csr,
     ps, pr, us, ur, vs, vr, own,
 ):
@@ -270,29 +270,32 @@
 
     lane = lax.broadcasted_iota(jnp.int32, (1, 128), 1)
     RB, CB, SB = R // 128, C // 128, WIDE // 128
-    block = 128
-
-    def row_pass(pot, weights):
+    block = Y * nb
+
+    def row_block(pot, weights, i):
         def shift(j):
             return jnp.concatenate([pot[j * SB + t:j * SB + t + 1] for t in range(SB)], axis=1)
 
+        rows = pl.ds(pl.multiple_of(i * block, block), block)
+        vals = [score[j, rows, :] + (0.0 if pot is None else shift(j))
+                for j in range(NB)]
+        peak = functools.reduce(jnp.maximum, vals)
+        peak = jnp.max(peak, axis=1, keepdims=True)
+        exps = [jnp.exp(v - peak) for v in vals]
+        total = jnp.sum(functools.reduce(jnp.add, exps), axis=1, keepdims=True)
+        st[rows, :] = jnp.where(lane == 0, peak, total)
+        if weights:
+            for j in range(NB):
+                h, l = split(exps[j])
+                wh[rows, j * WIDE:(j + 1) * WIDE] = h
+                wl[rows, j * WIDE:(j + 1) * WIDE] = l
+
+    def row_pass(pot):
         def body(i, carry):
-            rows = pl.ds(pl.multiple_of(i * block, block), block)
-            vals = [score[j, rows, :] + (0.0 if pot is None else shift(j))
-                    for j in range(NB)]
-            peak = functools.reduce(jnp.maximum, vals)
-            peak = jnp.max(peak, axis=1, keepdims=True)
-            exps = [jnp.exp(v - peak) for v in vals]
-            total = jnp.sum(functools.reduce(jnp.add, exps), axis=1, keepdims=True)
-            st[rows, :] = jnp.where(lane == 0, peak, total)
-            if weights:
-                for j in range(NB):
-                    h, l = split(exps[j])
-                    wh[rows, j * WIDE:(j + 1) * WIDE] = h
-                    wl[rows, j * WIDE:(j + 1) * WIDE] = l
+            row_block(pot, False, i)
             return carry
 
-        lax.fori_loop(0, R // block, body, 0)
+        lax.fori_loop(0, Z, body, 0)
 
     def row_copy(ex, r, landed=False):
         g2 = lax.rem(g + r, G)
@@ -320,16 +323,16 @@
         at = q2 if landed else q
         return rc(cs.at[ex, at], cs.at[ex, at], css.at[ex, r], csr.at[ex, at], quad_dev(q2))
 
-    def spread(packed):
+    def spread(ref, packed):
         for k in range(RB):
-            st[k * 128:(k + 1) * 128, :] = jnp.broadcast_to(packed[k:k + 1], (128, 128)).T
+            ref[k * 128:(k + 1) * 128, :] = jnp.broadcast_to(packed[k:k + 1], (128, 128)).T
 
     pot = None
     for step in range(ITERS):
-        row_pass(pot, False)
+        row_pass(pot)
         row_exchange(step)
         top, total = row_combine(step)
-        spread(math.log(total_data) - (top + jnp.log(total)))
+        spread(st, math.log(total_data) - (top + jnp.log(total)))
         for j in range(NB):
             for t in range(SB):
                 lanes, at = slice(t * 128, (t + 1) * 128), j * SB + t
@@ -347,8 +350,6 @@
         total = sum(cs[step, k, CB:2 * CB, :] * jnp.exp(peaks[k] - top) for k in range(QUAD))
         pot = math.log(total_noise) - (top + jnp.log(total))
 
-    row_pass(pot, True)
-    row_exchange(ITERS)
     main = nb - TAIL
     cutat = -(-main // (8 * HALVES)) * 8
     pieces = [pl.ds(0, cutat), pl.ds(cutat, main - cutat)]
@@ -376,7 +377,7 @@
         return rc(part.at[zz, :, tail], dt.at[zz], vs.at[zz, HALVES], vr.at[zz, HALVES],
                   dev(z - 1, y, x, c))
 
-    def multiply(zz, scaled):
+    def multiply(zz):
         rows = pl.ds(pl.multiple_of(zz * (Y * nb), Y * nb), Y * nb)
         both = jnp.concatenate([wh[rows, :], wl[rows, :]], axis=0)
         for n in range(D // 256):
@@ -384,8 +385,6 @@
             numer = dot3_stacked(both, dh[:, lanes], dl[:, lanes], NN)
             for t in range(2):
                 piece = numer[:, t * 128:(t + 1) * 128]
-                if scaled:
-                    piece = piece * st[rows, :]
                 for k in range(Y):
                     part[zz, k, :, n * 256 + t * 128:n * 256 + (t + 1) * 128] = (
                         piece[k * nb:(k + 1) * nb])
@@ -394,25 +393,37 @@
         for h in range(HALVES):
             for r in range(1, Y):
                 part_copy(zz, h, r).start()
-        pl.when((zz > z) & (z == 0))(lambda: up_tail(zz).start())
-        pl.when((zz < z) & (z == Z - 1))(lambda: dn_tail(zz).start())
+
+    def weigh(n, carry):
+        row_block(pot, True, order(n))
+        return carry
 
     first = order(jnp.int32(0))
-    multiply(first, False)
-    top, total = row_combine(ITERS)
-    spread(jnp.exp(rs[ITERS, g, 0:RB, :] - top) / total)
-    for k in range(Y):
-        scale = st[pl.ds(pl.multiple_of(first * (Y * nb), Y * nb) + k * nb, nb), :]
-        for t in range(D // 128):
-            part[first, k, :, t * 128:(t + 1) * 128] *= scale
+    weigh(jnp.int32(0), 0)
+    multiply(first)
     launch(first)
+    lax.fori_loop(1, Z, weigh, 0)
+    row_exchange(ITERS)
 
     def multiply_body(n, carry):
-        multiply(order(n), True)
+        multiply(order(n))
         launch(order(n))
         return carry
 
     lax.fori_loop(1, Z, multiply_body, 0)
+    top, total = row_combine(ITERS)
+    for k in range(Y):
+        spread(sc.at[k], jnp.exp(rs[ITERS, z * Y + k, 0:RB, :] - top) / total)
+
+    def tail_scale(i, carry):
+        zz, k = lax.div(i, Y), lax.rem(i, Y)
+        scale = sc[y, pl.ds(pl.multiple_of(i * nb + main, 8), TAIL), :]
+        for t in range(D // 128):
+            lanes = slice(t * 128, (t + 1) * 128)
+            part[zz, k, tail, lanes] = part[zz, k, tail, lanes] * scale
+        return carry
+
+    lax.fori_loop(0, G, tail_scale, 0)
 
     def tail_body(n, carry):
         zz = order(n)
@@ -427,8 +438,8 @@
             dn_tail(zz).wait_recv()
             part[zz, :, tail, :] += dt[zz]
 
-        pl.when((zz > z) & (z > 0))(lambda: up_tail(zz).start())
-        pl.when((zz < z) & (z + 1 < Z))(lambda: dn_tail(zz).start())
+        pl.when(zz > z)(lambda: up_tail(zz).start())
+        pl.when(zz < z)(lambda: dn_tail(zz).start())
 
         @pl.when(zz == z)
         def _():
@@ -439,42 +450,6 @@
 
     lax.fori_loop(0, Z, tail_body, 0)
 
-    def reduce_body(n, carry):
-        zz = order(n)
-        for h, rows in enumerate(pieces):
-            for r in range(1, Y):
-                part_copy(zz, h, r, True).wait_recv()
-                part[zz, y, rows, :] += yb[zz, lax.rem(y + r, Y), rows, :]
-
-            @pl.when((zz >= z) & (z > 0))
-            def _():
-                up_part(zz, h).wait_recv()
-                part[zz, y, rows, :] += ub[zz, rows, :]
-
-            @pl.when((zz <= z) & (z + 1 < Z))
-            def _():
-                dn_part(zz, h).wait_recv()
-                part[zz, y, rows, :] += db[zz, rows, :]
-
-            pl.when(zz > z)(lambda: up_part(zz, h).start())
-            pl.when(zz < z)(lambda: dn_part(zz, h).start())
-        return carry
-
-    lax.fori_loop(0, Z, reduce_body, 0)
-    for r in range(1, Y):
-        part_copy(z, HALVES, r, True).wait_recv()
-        part[z, y, tail, :] += yb[z, lax.rem(y + r, Y), tail, :]
-
-    wide_times = jnp.concatenate([times_ref[...], jnp.zeros((1, 128 - nb), f32)], axis=1)
-    share = jnp.broadcast_to(wide_times, (128, 128)).T[0:nb]
-    for t in range(D // 128):
-        lanes = slice(t * 128, (t + 1) * 128)
-        noise, targets = nf[g, :, lanes], part[z, y, :, lanes]
-        path_ref[:, lanes] = (1.0 - share) * noise + share * targets
-        velocity_ref[:, lanes] = targets - noise
-
-    for r in range(1, Y):
-        part_copy(z, HALVES, r).wait_send()
     for k in range(PIECES):
         data_send(k).wait_send()
         data_forward(k).wait_send()
@@ -491,6 +466,45 @@
     for zz in range(Z):
         for r in range(1, Y):
             y_copy(zz, r).wait_send()
+
+    def reduce_body(n, carry):
+        zz = order(n)
+        for h, rows in enumerate(pieces):
+            for r in range(1, Y):
+                part_copy(zz, h, r, True).wait_recv()
+            base = pl.multiple_of(zz * (Y * nb) + y * nb + rows.start, 8)
+            scales = [sc[lax.rem(y + r, Y), pl.ds(base, rows.size), :] for r in range(Y)]
+            for t in range(D // 128):
+                lanes = slice(t * 128, (t + 1) * 128)
+                value = part[zz, y, rows, lanes] * scales[0]
+                for r in range(1, Y):
+                    value += yb[zz, lax.rem(y + r, Y), rows, lanes] * scales[r]
+                part[zz, y, rows, lanes] = value
+
+            @pl.when((zz >= z) & (z > 0))
+            def _():
+                up_part(zz, h).wait_recv()
+                part[zz, y, rows, :] += ub[zz, rows, :]
+
+            @pl.when((zz <= z) & (z + 1 < Z))
+            def _():
+                dn_part(zz, h).wait_recv()
+                part[zz, y, rows, :] += db[zz, rows, :]
+
+            pl.when(zz > z)(lambda: up_part(zz, h).start())
+            pl.when(zz < z)(lambda: dn_part(zz, h).start())
+        return carry
+
+    lax.fori_loop(0, Z, reduce_body, 0)
+    for r in range(1, Y):
+        part_copy(z, HALVES, r, True).wait_recv()
+        part[z, y, tail, :] += yb[z, lax.rem(y + r, Y), tail, :]
+
+    out_ref[...] = part[z, y]
+
+    for r in range(1, Y):
+        part_copy(z, HALVES, r).wait_send()
+    for zz in range(Z):
         for h in range(HALVES):
             for r in range(1, Y):
                 part_copy(zz, h, r).wait_send()
@@ -500,7 +514,7 @@
         pl.when(zz < z)(lambda: dn_tail(zz).wait_send())
 
 
-def per_device(Z, Y, noise, data, times):
+def targets_of(Z, Y, noise, data):
     nb, D = noise.shape
     md = data.shape[0]
     G = Z * Y
@@ -509,9 +523,9 @@
     flops = 2 * 6 * R * C * D
     return pl.pallas_call(
         functools.partial(kernel, Z, Y),
-        out_shape=[jax.ShapeDtypeStruct((nb, D), f32)] * 2,
-        in_specs=[pl.BlockSpec(memory_space=pl.ANY)] * 2 + [pl.BlockSpec(memory_space=pltpu.VMEM)],
-        out_specs=[pl.BlockSpec(memory_space=pltpu.VMEM)] * 2,
+        out_shape=jax.ShapeDtypeStruct((nb, D), f32),
+        in_specs=[pl.BlockSpec(memory_space=pl.ANY)] * 2,
+        out_specs=pl.BlockSpec(memory_space=pltpu.VMEM),
         scratch_shapes=[
             V((G, nb, D), f32), V((QUAD, md, D), f32),
             V((R, D), bf16), V((R, D), bf16), V((C, D), bf16), V((C, D), bf16),
@@ -520,7 +534,7 @@
             V((R, C), bf16), V((R, C), bf16),
             V((ITERS + 1, G, R // 64, 128), f32), V((ITERS, QUAD, C // 64, 128), f32),
             V((Z, Y, nb, D), f32), V((Z, Y, nb, D), f32), V((Z, nb, D), f32), V((Z, nb, D), f32),
-            V((Z, Y, TAIL, D), f32), V((Z, Y, TAIL, D), f32),
+            V((Z, Y, TAIL, D), f32), V((Z, Y, TAIL, D), f32), V((Y, R, 128), f32),
             dma((Z,)), dma((Z,)), dma((Z,)), dma((Z,)),
             dma((Z, Y)), dma((Z, Y)),
             dma((PIECES,)), dma((PIECES,)), dma((2,)), dma((PIECES,)), dma((PIECES,)),
@@ -533,7 +547,13 @@
             collective_id=0, has_side_effects=True, vmem_limit_bytes=60 * 1024 * 1024),
         cost_estimate=pl.CostEstimate(
             flops=flops, bytes_accessed=8 * (R + C) * D, transcendentals=5 * R * C),
-    )(noise, data, times.reshape(1, nb))
+    )(noise, data)
+
+
+def per_device(Z, Y, noise, data, times):
+    targets = targets_of(Z, Y, noise, data)
+    path = (1.0 - times)[:, None] * noise + times[:, None] * targets
+    return (path, targets - noise)
 
 
 def solution(mesh):

time: 137 us -> 143 us (1.044)
  Pallas kernels: 132 us -> 140 us
  local copies, waits for them, and re-layouts: 3.74 us -> 0.01 us
  other arithmetic: 0 us -> 2.73 us
    pallas_call x1, Pallas kernels: 132 us -> 140 us  [targets_of(): pl.pallas_call(functools.partial(kernel, Z, Y), out_shape=jax.ShapeDtypeS...]
    unnamed x2 -> x4, local copies, waits for them, and re-layouts: 3.74 us -> 0.01 us
    sub x0 -> x2, other arithmetic: none -> 2.73 us  [the longest x1 2.07 us: per_device(): return (path, targets - noise)]
where the time goes in v6:
time: 143 us
  Pallas kernels  140 us (98%)
  other arithmetic  2.73 us (2%)
    pallas_call x1, Pallas kernels, targets_of(): pl.pallas_call(functools.partial(kernel, Z, Y), out_shape=jax.ShapeDtypeS...  140 us

profile of v6, /device:TPU:0, one launch (start us, length us, event | category | flops | bytes accessed | tf_op | source)
XLA Modules:
  0.0 143.1 jit_solution(10479353173644111019)
XLA Ops:
  0.6 0.7 broadcast_subtract_fusion
  1.3 0.0 copy-start
  1.3 0.0 copy-start.1
  1.3 139.7 %shard_map.50 = f32[64,2048]{1,0:T(8,128)} custom-call(f32[64,2048]{1,0:T(8,128)} %noise_ref.1, f32[256,2048]{1,0:T(8,128)} %data_ref.1), custom_call_target="tpu_custom_call" | custom-call | flops 12884901888 | bytes 25165824 | tf_op jit(solution)/shard_map/pallas_call | solution.py:524
  141.0 0.0 copy-done
  141.0 0.0 copy-done.1
  141.0 2.1 %fusion = (f32[64,2048]{1,0:T(8,128)}, f32[64,2048]{1,0:T(8,128)}) fusion(f32[64,2048]{1,0:T(8,128)} %shard_map.50, f32[64,2048]{1,0:T(8,128)S(1)} %copy-done, f32[64]{0:T(128)S(1)} %copy-done.1, f32[64]{0:T(128)S(1)} %broadcast_subtract_fusion), kind=kLoop, calls=%fused_computation.2 | loop fusion | flops 524288 | bytes 2097664 | tf_op jit(solution)/shard_map/sub | solution.py:556
Async XLA Ops:
  1.3 139.7 %copy-start = (f32[64,2048]{1,0:T(8,128)S(1)}, f32[64,2048]{1,0:T(8,128)}, u32[]{:S(2)}) copy-start(f32[64,2048]{1,0:T(8,128)} %noise_ref.1) | copy-start | bytes 1572868
  1.3 139.7 %copy-start.1 = (f32[64]{0:T(128)S(1)}, f32[64]{0:T(128)}, u32[]{:S(2)}) copy-start(f32[64]{0:T(128)} %param.5) | copy-start | bytes 772

commit v7 on v6

--- a/solution.py
+++ b/solution.py
@@ -15,7 +15,6 @@
 QUAD = PAIR * CORES
 WIDE = 128 * CORES
 PIECES = 4
-TAIL = 8
 HALVES = 2
 f32 = jnp.float32
 bf16 = jnp.bfloat16
@@ -42,7 +41,7 @@
 
 def kernel(
     Z, Y, noise_ref, data_ref, out_ref,
-    nf, df, nh, nl, dh, dl, rn, cn, score, st, wh, wl, rs, cs, part, yb, ub, db, ut, dt, sc,
+    nf, df, nh, nl, dh, dl, rn, cn, score, st, wh, wl, rs, cs, part, yb, ub, db, sc,
     up_s, up_r, dn_s, dn_r, ys, yr, xs, xr, sib, fs, fr, rss, rsr, css, csr,
     ps, pr, us, ur, vs, vr, own,
 ):
@@ -350,14 +349,12 @@
         total = sum(cs[step, k, CB:2 * CB, :] * jnp.exp(peaks[k] - top) for k in range(QUAD))
         pot = math.log(total_noise) - (top + jnp.log(total))
 
-    main = nb - TAIL
-    cutat = -(-main // (8 * HALVES)) * 8
-    pieces = [pl.ds(0, cutat), pl.ds(cutat, main - cutat)]
-    tail = pl.ds(main, TAIL)
+    cutat = -(-nb // (8 * HALVES)) * 8
+    pieces = [pl.ds(h * cutat, min(cutat, nb - h * cutat)) for h in range(HALVES)]
 
     def part_copy(zz, h, r, landed=False):
         y2 = lax.rem(y + r, Y)
-        rows, at = (pieces + [tail])[h], y2 if landed else y
+        rows, at = pieces[h], y2 if landed else y
         return rc(part.at[zz, y2, rows], yb.at[zz, at, rows],
                   ps.at[zz, h, r], pr.at[zz, h, at], dev(z, y2, x, c))
 
@@ -367,14 +364,6 @@
 
     def dn_part(zz, h):
         return rc(part.at[zz, y, pieces[h]], db.at[zz, pieces[h]], vs.at[zz, h], vr.at[zz, h],
-                  dev(z - 1, y, x, c))
-
-    def up_tail(zz):
-        return rc(part.at[zz, :, tail], ut.at[zz], us.at[zz, HALVES], ur.at[zz, HALVES],
-                  dev(z + 1, y, x, c))
-
-    def dn_tail(zz):
-        return rc(part.at[zz, :, tail], dt.at[zz], vs.at[zz, HALVES], vr.at[zz, HALVES],
                   dev(z - 1, y, x, c))
 
     def multiply(zz):
@@ -414,41 +403,6 @@
     top, total = row_combine(ITERS)
     for k in range(Y):
         spread(sc.at[k], jnp.exp(rs[ITERS, z * Y + k, 0:RB, :] - top) / total)
-
-    def tail_scale(i, carry):
-        zz, k = lax.div(i, Y), lax.rem(i, Y)
-        scale = sc[y, pl.ds(pl.multiple_of(i * nb + main, 8), TAIL), :]
-        for t in range(D // 128):
-            lanes = slice(t * 128, (t + 1) * 128)
-            part[zz, k, tail, lanes] = part[zz, k, tail, lanes] * scale
-        return carry
-
-    lax.fori_loop(0, G, tail_scale, 0)
-
-    def tail_body(n, carry):
-        zz = order(n)
-
-        @pl.when((zz >= z) & (z > 0))
-        def _():
-            up_tail(zz).wait_recv()
-            part[zz, :, tail, :] += ut[zz]
-
-        @pl.when((zz <= z) & (z + 1 < Z))
-        def _():
-            dn_tail(zz).wait_recv()
-            part[zz, :, tail, :] += dt[zz]
-
-        pl.when(zz > z)(lambda: up_tail(zz).start())
-        pl.when(zz < z)(lambda: dn_tail(zz).start())
-
-        @pl.when(zz == z)
-        def _():
-            for r in range(1, Y):
-                part_copy(zz, HALVES, r).start()
-
-        return carry
-
-    lax.fori_loop(0, Z, tail_body, 0)
 
     for k in range(PIECES):
         data_send(k).wait_send()
@@ -496,22 +450,14 @@
         return carry
 
     lax.fori_loop(0, Z, reduce_body, 0)
-    for r in range(1, Y):
-        part_copy(z, HALVES, r, True).wait_recv()
-        part[z, y, tail, :] += yb[z, lax.rem(y + r, Y), tail, :]
-
     out_ref[...] = part[z, y]
 
-    for r in range(1, Y):
-        part_copy(z, HALVES, r).wait_send()
     for zz in range(Z):
         for h in range(HALVES):
             for r in range(1, Y):
                 part_copy(zz, h, r).wait_send()
             pl.when(zz > z)(lambda: up_part(zz, h).wait_send())
             pl.when(zz < z)(lambda: dn_part(zz, h).wait_send())
-        pl.when(zz > z)(lambda: up_tail(zz).wait_send())
-        pl.when(zz < z)(lambda: dn_tail(zz).wait_send())
 
 
 def targets_of(Z, Y, noise, data):
@@ -534,14 +480,14 @@
             V((R, C), bf16), V((R, C), bf16),
             V((ITERS + 1, G, R // 64, 128), f32), V((ITERS, QUAD, C // 64, 128), f32),
             V((Z, Y, nb, D), f32), V((Z, Y, nb, D), f32), V((Z, nb, D), f32), V((Z, nb, D), f32),
-            V((Z, Y, TAIL, D), f32), V((Z, Y, TAIL, D), f32), V((Y, R, 128), f32),
+            V((Y, R, 128), f32),
             dma((Z,)), dma((Z,)), dma((Z,)), dma((Z,)),
             dma((Z, Y)), dma((Z, Y)),
             dma((PIECES,)), dma((PIECES,)), dma((2,)), dma((PIECES,)), dma((PIECES,)),
             dma((ITERS + 1, G)), dma((ITERS + 1, G)), dma((ITERS, QUAD)), dma((ITERS, QUAD)),
-            dma((Z, HALVES + 1, Y)), dma((Z, HALVES + 1, Y)),
-            dma((Z, HALVES + 1)), dma((Z, HALVES + 1)),
-            dma((Z, HALVES + 1)), dma((Z, HALVES + 1)), dma((2,)),
+            dma((Z, HALVES, Y)), dma((Z, HALVES, Y)),
+            dma((Z, HALVES)), dma((Z, HALVES)),
+            dma((Z, HALVES)), dma((Z, HALVES)), dma((2,)),
         ],
         compiler_params=pltpu.CompilerParams(
             collective_id=0, has_side_effects=True, vmem_limit_bytes=60 * 1024 * 1024),

time: 143 us -> 137 us (0.958)
  Pallas kernels: 140 us -> 133 us
    pallas_call x1, Pallas kernels: 140 us -> 133 us  [targets_of(): pl.pallas_call(functools.partial(kernel, Z, Y), out_shape=jax.ShapeDtypeS...]
where the time goes in v7:
time: 137 us
  Pallas kernels  133 us (97%)
  other arithmetic  2.73 us (2%)
    pallas_call x1, Pallas kernels, targets_of(): pl.pallas_call(functools.partial(kernel, Z, Y), out_shape=jax.ShapeDtypeS...  133 us

profile of v7, /device:TPU:0, one launch (start us, length us, event | category | flops | bytes accessed | tf_op | source)
XLA Modules:
  0.0 136.8 jit_solution(3309992410293458700)
XLA Ops:
  0.6 0.7 broadcast_subtract_fusion
  1.3 0.0 copy-start
  1.3 0.0 copy-start.1
  1.3 133.4 %shard_map.50 = f32[64,2048]{1,0:T(8,128)} custom-call(f32[64,2048]{1,0:T(8,128)} %noise_ref.1, f32[256,2048]{1,0:T(8,128)} %data_ref.1), custom_call_target="tpu_custom_call" | custom-call | flops 12884901888 | bytes 25165824 | tf_op jit(solution)/shard_map/pallas_call | solution.py:470
  134.7 0.0 copy-done
  134.8 0.0 copy-done.1
  134.8 2.1 %fusion = (f32[64,2048]{1,0:T(8,128)}, f32[64,2048]{1,0:T(8,128)}) fusion(f32[64,2048]{1,0:T(8,128)} %shard_map.50, f32[64,2048]{1,0:T(8,128)S(1)} %copy-done, f32[64]{0:T(128)S(1)} %copy-done.1, f32[64]{0:T(128)S(1)} %broadcast_subtract_fusion), kind=kLoop, calls=%fused_computation.2 | loop fusion | flops 524288 | bytes 2097664 | tf_op jit(solution)/shard_map/sub | solution.py:502
Async XLA Ops:
  1.3 133.5 %copy-start = (f32[64,2048]{1,0:T(8,128)S(1)}, f32[64,2048]{1,0:T(8,128)}, u32[]{:S(2)}) copy-start(f32[64,2048]{1,0:T(8,128)} %noise_ref.1) | copy-start | bytes 1572868
  1.3 133.5 %copy-start.1 = (f32[64]{0:T(128)S(1)}, f32[64]{0:T(128)}, u32[]{:S(2)}) copy-start(f32[64]{0:T(128)} %param.5) | copy-start | bytes 772

commit v8 on v7

--- a/solution.py
+++ b/solution.py
@@ -396,7 +396,6 @@
 
     def multiply_body(n, carry):
         multiply(order(n))
-        launch(order(n))
         return carry
 
     lax.fori_loop(1, Z, multiply_body, 0)
@@ -426,6 +425,12 @@
         for h, rows in enumerate(pieces):
             for r in range(1, Y):
                 part_copy(zz, h, r, True).wait_recv()
+
+            @pl.when(n + 1 < Z)
+            def _():
+                for r in range(1, Y):
+                    part_copy(order(n + 1), h, r).start()
+
             base = pl.multiple_of(zz * (Y * nb) + y * nb + rows.start, 8)
             scales = [sc[lax.rem(y + r, Y), pl.ds(base, rows.size), :] for r in range(Y)]
             for t in range(D // 128):

time: 137 us -> 138 us (level)
  no operation moved by 1% of the time
where the time goes in v8:
time: 138 us; the launch traced here: 137 us
  Pallas kernels  134 us (97%)
  other arithmetic  2.73 us (2%)
    pallas_call x1, Pallas kernels, targets_of(): pl.pallas_call(functools.partial(kernel, Z, Y), out_shape=jax.ShapeDtypeS...  134 us

profile of v8, /device:TPU:0, one launch (start us, length us, event | category | flops | bytes accessed | tf_op | source)
XLA Modules:
  0.0 137.4 jit_solution(10261408791568686904)
XLA Ops:
  0.6 0.7 broadcast_subtract_fusion
  1.3 0.0 copy-start
  1.3 0.0 copy-start.1
  1.3 134.0 %shard_map.50 = f32[64,2048]{1,0:T(8,128)} custom-call(f32[64,2048]{1,0:T(8,128)} %noise_ref.1, f32[256,2048]{1,0:T(8,128)} %data_ref.1), custom_call_target="tpu_custom_call" | custom-call | flops 12884901888 | bytes 25165824 | tf_op jit(solution)/shard_map/pallas_call | solution.py:475
  135.3 0.0 copy-done
  135.3 0.0 copy-done.1
  135.3 2.1 %fusion = (f32[64,2048]{1,0:T(8,128)}, f32[64,2048]{1,0:T(8,128)}) fusion(f32[64,2048]{1,0:T(8,128)} %shard_map.50, f32[64,2048]{1,0:T(8,128)S(1)} %copy-done, f32[64]{0:T(128)S(1)} %copy-done.1, f32[64]{0:T(128)S(1)} %broadcast_subtract_fusion), kind=kLoop, calls=%fused_computation.2 | loop fusion | flops 524288 | bytes 2097664 | tf_op jit(solution)/shard_map/sub | solution.py:507
Async XLA Ops:
  1.3 134.0 %copy-start = (f32[64,2048]{1,0:T(8,128)S(1)}, f32[64,2048]{1,0:T(8,128)}, u32[]{:S(2)}) copy-start(f32[64,2048]{1,0:T(8,128)} %noise_ref.1) | copy-start | bytes 1572868
  1.3 134.0 %copy-start.1 = (f32[64]{0:T(128)S(1)}, f32[64]{0:T(128)}, u32[]{:S(2)}) copy-start(f32[64]{0:T(128)} %param.5) | copy-start | bytes 772
